TPU v7x, 256 devices: a whole 4x4x8 slice. The times are simulated.
256 devices in a mesh: dp: 2 (over x_lo), ctx: 128 (over x_hi, y, z, core).
Axes of the slice: x: 4 (x_hi: 2, x_lo: 2; x = x_hi * 2 + x_lo), y: 4, z: 8, core: 2. Of those that a mesh axis runs over, the one named last changes fastest.
Arguments:
- features: bfloat16 [2, 16384, 1536], P('dp', 'ctx'), may hold values from -500 to 500
- gain: float32 [1536], replicated, may hold values from 0.1 to 1.9
- conv_weight: bfloat16 [5, 1536, 768], replicated, may hold values from -0.0625 to 0.0625
- cotangent: bfloat16 [2, 16384, 768], P('dp', 'ctx'), may hold values from -15 to 15
Outputs:
- convolved: bfloat16 [2, 16384, 768], P('dp', 'ctx')
- input_grad: bfloat16 [2, 16384, 1536], P('dp', 'ctx')
- gain_grad: float32 [1536], replicated
All inputs are finite; a program needn't handle non-finite values.
Results may differ from a plain program's by a relative error of at most 0.0054.
Values may be sent and summed in bfloat16 or wider, within the bound.
No kernel may reach another device: no remote copies, remote signals or barrier semaphores. Data moves between devices by JAX's collectives and lax.ppermute only.
A program may use at most 64 MiB of HBM per device.

v0:
```python
import math

import jax
import jax.numpy as jnp
from jax import lax
from jax.sharding import PartitionSpec as P

KERNEL_TAPS = 5


EPS = 1e-06


def shifted(block, axis, distance):
    devices = range(lax.axis_size(axis))
    route = [(i - distance, i) for i in devices if i - distance in devices]
    return lax.ppermute(block, axis, route)


def partner(value, axis, apart):
    mask = 2**apart
    pairs = [(source, source ^ mask) for source in range(lax.axis_size(axis))]
    return lax.ppermute(value, axis, pairs)


def activate(values):
    return jax.nn.gelu(values, approximate=True)


def flip_both(values):
    return values[:, ::-1, ::-1]


def bit_list(count):
    return list(range(count))


def bit_count():
    return lax.axis_size("ctx").bit_length() - 1


def taps_ahead(values, shard_hops):
    pieces = []
    for tap_index in range(KERNEL_TAPS):
        if tap_index == KERNEL_TAPS // 2:
            pieces.append(values)
        else:
            pieces.append(shifted(values, "ctx", -(tap_index - KERNEL_TAPS // 2) * shard_hops))
    return pieces


def taps_behind(values, shard_hops):
    pieces = []
    for tap_index in range(KERNEL_TAPS):
        if tap_index == KERNEL_TAPS // 2:
            pieces.append(values)
        else:
            pieces.append(shifted(values, "ctx", (tap_index - KERNEL_TAPS // 2) * shard_hops))
    return pieces


def mirrored_ahead(values, shard_hops):
    pieces = []
    for tap_index in range(KERNEL_TAPS):
        if tap_index == KERNEL_TAPS // 2:
            pieces.append(values)
        else:
            pieces.append(shifted(values, "ctx", -(tap_index - KERNEL_TAPS // 2) * shard_hops))
    return pieces


def mirrored_behind(values, shard_hops):
    pieces = []
    for tap_index in range(KERNEL_TAPS):
        if tap_index == KERNEL_TAPS // 2:
            pieces.append(values)
        else:
            pieces.append(shifted(values, "ctx", (tap_index - KERNEL_TAPS // 2) * shard_hops))
    return pieces


def mirror_acts(values):
    for bit_number in bit_list(bit_count()):
        values = partner(values, "ctx", bit_number)
    return values


def mirror_out(values):
    for bit_number in bit_list(bit_count()):
        values = partner(values, "ctx", bit_number)
    return values


def mirror_grads(values):
    for bit_number in bit_list(bit_count()):
        values = partner(values, "ctx", bit_number)
    return values


def reflect_backward(values):
    for bit_number in bit_list(bit_count()):
        values = partner(values, "ctx", bit_number)
    return values


def apply_forward(pieces, weight):
    lead = pieces[0].shape[0]
    middle = pieces[0].shape[1]
    total = jnp.zeros((lead * middle, weight.shape[2]), jnp.float32)
    for tap_index in range(KERNEL_TAPS):
        flat_rows = pieces[tap_index].reshape(lead * middle, pieces[tap_index].shape[2])
        total = total + jnp.dot(flat_rows, weight[tap_index], preferred_element_type=jnp.float32)
    return total.reshape(lead, middle, weight.shape[2])


def apply_backward(pieces, weight):
    lead = pieces[0].shape[0]
    middle = pieces[0].shape[1]
    total = jnp.zeros((lead * middle, weight.shape[1]), jnp.float32)
    for tap_index in range(KERNEL_TAPS):
        flat_rows = pieces[tap_index].reshape(lead * middle, pieces[tap_index].shape[2])
        total = total + lax.dot_general(
            flat_rows,
            weight[tap_index],
            (((1,), (1,)), ((), ())),
            preferred_element_type=jnp.float32,
        )
    return total.reshape(lead, middle, weight.shape[1])


def per_device(features, gain, conv_weight, cotangent):
    shard_hops = lax.axis_size("ctx") // 8
    wide = features.astype(jnp.float32)
    inv_rms = lax.rsqrt(jnp.mean(wide * wide, axis=-1, keepdims=True) + EPS)
    normed = wide * inv_rms
    scaled = normed * gain
    hidden = activate(scaled).astype(jnp.bfloat16)
    ahead = taps_ahead(hidden, shard_hops)
    forward_term = apply_forward(ahead, conv_weight)
    turned_input = flip_both(mirror_acts(hidden))
    turned = apply_forward(mirrored_ahead(turned_input, shard_hops), conv_weight).astype(
        jnp.bfloat16
    )
    reverse_term = flip_both(mirror_out(turned))
    convolved = (forward_term + reverse_term.astype(jnp.float32)).astype(jnp.bfloat16)
    behind = taps_behind(cotangent, shard_hops)
    back_forward = apply_backward(behind, conv_weight)
    turned_grads = flip_both(mirror_grads(cotangent))
    back_turned = apply_backward(mirrored_behind(turned_grads, shard_hops), conv_weight).astype(
        jnp.bfloat16
    )
    back_reverse = flip_both(reflect_backward(back_turned))
    grad_hidden = back_forward + back_reverse.astype(jnp.float32)
    _, pullback = jax.vjp(activate, scaled)
    grad_scaled = pullback(grad_hidden)[0]
    partial_sum = jnp.sum(grad_scaled * normed, axis=(0, 1))
    summed = lax.psum(partial_sum, ("dp", "ctx"))
    total_rows = features.shape[0] * features.shape[1] * lax.axis_size("dp") * lax.axis_size("ctx")
    gain_grad = summed / math.sqrt(total_rows)
    grad_normed = grad_scaled * gain
    spread_term = jnp.mean(grad_normed * normed, axis=-1, keepdims=True)
    input_grad = (inv_rms * (grad_normed - normed * spread_term)).astype(jnp.bfloat16)
    return (convolved, input_grad, gain_grad)


def solution(mesh):
    return jax.shard_map(
        per_device,
        mesh=mesh,
        in_specs=(P("dp", "ctx", None), P(), P(), P("dp", "ctx", None)),
        out_specs=(P("dp", "ctx", None), P("dp", "ctx", None), P()),
        check_vma=False,
    )
```

profile of v0, /device:TPU:1, one launch (start us, length us, event | category | flops | bytes accessed | tf_op | source)
XLA Modules:
  0.0 472.8 jit_solution(13395752870497047285)
XLA Ops:
  5.3 6.1 %collective-permute-done.27 = bf16[1,128,768]{2,1,0:T(8,128)(2,1)S(1)} collective-permute-done((bf16[1,128,768]{2,1,0:T(8,128)(2,1)S(1)}, bf16[1,128,768]{2,1,0:T(8,128)(2,1)S(1)}, u32[]{:S(2)}, u32[]{:S(2)}) %collective-permute-start.27) | collective-permute-done | bytes 196640 | tf_op jit(solution)/shard_map/ppermute | solution.py:23
  13.0 10.1 %collective-permute-done.28 = bf16[1,128,768]{2,1,0:T(8,128)(2,1)S(1)} collective-permute-done((bf16[1,128,768]{2,1,0:T(8,128)(2,1)S(1)}, bf16[1,128,768]{2,1,0:T(8,128)(2,1)S(1)}, u32[]{:S(2)}, u32[]{:S(2)}) %collective-permute-start.28) | collective-permute-done | bytes 196640 | tf_op jit(solution)/shard_map/ppermute | solution.py:23
  28.0 7.9 %collective-permute-done.29 = bf16[1,128,768]{2,1,0:T(8,128)(2,1)S(1)} collective-permute-done((bf16[1,128,768]{2,1,0:T(8,128)(2,1)S(1)}, bf16[1,128,768]{2,1,0:T(8,128)(2,1)S(1)}, u32[]{:S(2)}, u32[]{:S(2)}) %collective-permute-start.29) | collective-permute-done | bytes 196640 | tf_op jit(solution)/shard_map/ppermute | solution.py:23
  60.3 6.1 %collective-permute-start.36 = (bf16[1,128,768]{2,1,0:T(8,128)(2,1)S(1)}, bf16[1,128,768]{2,1,0:T(8,128)(2,1)S(1)}, u32[]{:S(2)}, u32[]{:S(2)}) collective-permute-start(bf16[1,128,768]{2,1,0:T(8,128)(2,1)S(1)} %rev.14), channel_id=1, source_target_pairs={{0,32},{1,33},{2,34},{3,35},{4,36},{5,37},{6,38},{7,39},{8,40},{9,... | collective-permute-start | bytes 589832 | tf_op jit(solution)/shard_map/ppermute | solution.py:17
  78.8 5.8 %collective-permute-start.37 = (bf16[1,128,1536]{2,1,0:T(8,128)(2,1)S(1)}, bf16[1,128,1536]{2,1,0:T(8,128)(2,1)S(1)}, u32[]{:S(2)}, u32[]{:S(2)}) collective-permute-start(bf16[1,128,1536]{2,1,0:T(8,128)(2,1)S(1)} %fusion.42), channel_id=1, source_target_pairs={{0,1},{1,0},{2,3},{3,2},{4,5},{5,4},{6,7},{7,6},{8,9},{9,8},{10,11... | collective-permute-start | bytes 1179656 | tf_op jit(solution)/shard_map/ppermute | solution.py:23
  86.0 10.3 %collective-permute-done.38 = bf16[1,128,1536]{2,1,0:T(8,128)(2,1)S(1)} collective-permute-done((bf16[1,128,1536]{2,1,0:T(8,128)(2,1)S(1)}, bf16[1,128,1536]{2,1,0:T(8,128)(2,1)S(1)}, u32[]{:S(2)}, u32[]{:S(2)}) %collective-permute-start.38) | collective-permute-done | bytes 393248 | tf_op jit(solution)/shard_map/ppermute | solution.py:23
  98.9 17.1 %collective-permute-done.39 = bf16[1,128,1536]{2,1,0:T(8,128)(2,1)S(1)} collective-permute-done((bf16[1,128,1536]{2,1,0:T(8,128)(2,1)S(1)}, bf16[1,128,1536]{2,1,0:T(8,128)(2,1)S(1)}, u32[]{:S(2)}, u32[]{:S(2)}) %collective-permute-start.39) | collective-permute-done | bytes 393248 | tf_op jit(solution)/shard_map/ppermute | solution.py:23
  121.9 8.6 %collective-permute-start.25 = (bf16[1,128,768]{2,1,0:T(8,128)(2,1)S(1)}, bf16[1,128,768]{2,1,0:T(8,128)(2,1)S(1)}, u32[]{:S(2)}, u32[]{:S(2)}) collective-permute-start(bf16[1,128,768]{2,1,0:T(8,128)(2,1)S(1)} %copy-done.2), channel_id=1, source_target_pairs={{0,32},{1,33},{2,34},{3,35},{4,36},{5,37},{6,38},{7,39},{8,40},{9,... | collective-permute-start | bytes 589832 | tf_op jit(solution)/shard_map/ppermute | solution.py:17
  133.6 5.5 %collective-permute-done.40 = bf16[1,128,1536]{2,1,0:T(8,128)(2,1)S(1)} collective-permute-done((bf16[1,128,1536]{2,1,0:T(8,128)(2,1)S(1)}, bf16[1,128,1536]{2,1,0:T(8,128)(2,1)S(1)}, u32[]{:S(2)}, u32[]{:S(2)}) %collective-permute-start.40) | collective-permute-done | bytes 393248 | tf_op jit(solution)/shard_map/ppermute | solution.py:23
  144.1 7.8 %collective-permute-done.41 = bf16[1,128,1536]{2,1,0:T(8,128)(2,1)S(1)} collective-permute-done((bf16[1,128,1536]{2,1,0:T(8,128)(2,1)S(1)}, bf16[1,128,1536]{2,1,0:T(8,128)(2,1)S(1)}, u32[]{:S(2)}, u32[]{:S(2)}) %collective-permute-start.41) | collective-permute-done | bytes 393248 | tf_op jit(solution)/shard_map/ppermute | solution.py:23
  154.8 8.1 %collective-permute-done.42 = bf16[1,128,1536]{2,1,0:T(8,128)(2,1)S(1)} collective-permute-done((bf16[1,128,1536]{2,1,0:T(8,128)(2,1)S(1)}, bf16[1,128,1536]{2,1,0:T(8,128)(2,1)S(1)}, u32[]{:S(2)}, u32[]{:S(2)}) %collective-permute-start.42) | collective-permute-done | bytes 393248 | tf_op jit(solution)/shard_map/ppermute | solution.py:23
  165.5 7.5 %collective-permute-done.43 = bf16[1,128,1536]{2,1,0:T(8,128)(2,1)S(1)} collective-permute-done((bf16[1,128,1536]{2,1,0:T(8,128)(2,1)S(1)}, bf16[1,128,1536]{2,1,0:T(8,128)(2,1)S(1)}, u32[]{:S(2)}, u32[]{:S(2)}) %collective-permute-start.43) | collective-permute-done | bytes 393248 | tf_op jit(solution)/shard_map/ppermute | solution.py:23
  180.8 10.3 %collective-permute-done.5 = bf16[1,128,1536]{2,1,0:T(8,128)(2,1)S(1)} collective-permute-done((bf16[1,128,1536]{2,1,0:T(8,128)(2,1)S(1)}, bf16[1,128,1536]{2,1,0:T(8,128)(2,1)S(1)}, u32[]{:S(2)}, u32[]{:S(2)}) %collective-permute-start.5) | collective-permute-done | bytes 393248 | tf_op jit(solution)/shard_map/ppermute | solution.py:23
  194.3 17.1 %collective-permute-done.6 = bf16[1,128,1536]{2,1,0:T(8,128)(2,1)S(1)} collective-permute-done((bf16[1,128,1536]{2,1,0:T(8,128)(2,1)S(1)}, bf16[1,128,1536]{2,1,0:T(8,128)(2,1)S(1)}, u32[]{:S(2)}, u32[]{:S(2)}) %collective-permute-start.6) | collective-permute-done | bytes 393248 | tf_op jit(solution)/shard_map/ppermute | solution.py:23
  214.2 20.3 %collective-permute-done.7 = bf16[1,128,1536]{2,1,0:T(8,128)(2,1)S(1)} collective-permute-done((bf16[1,128,1536]{2,1,0:T(8,128)(2,1)S(1)}, bf16[1,128,1536]{2,1,0:T(8,128)(2,1)S(1)}, u32[]{:S(2)}, u32[]{:S(2)}) %collective-permute-start.7) | collective-permute-done | bytes 393248 | tf_op jit(solution)/shard_map/ppermute | solution.py:23
  235.4 9.3 %collective-permute-done.8 = bf16[1,128,1536]{2,1,0:T(8,128)(2,1)S(1)} collective-permute-done((bf16[1,128,1536]{2,1,0:T(8,128)(2,1)S(1)}, bf16[1,128,1536]{2,1,0:T(8,128)(2,1)S(1)}, u32[]{:S(2)}, u32[]{:S(2)}) %collective-permute-start.8) | collective-permute-done | bytes 393248 | tf_op jit(solution)/shard_map/ppermute | solution.py:23
  246.4 9.1 %collective-permute-done.9 = bf16[1,128,1536]{2,1,0:T(8,128)(2,1)S(1)} collective-permute-done((bf16[1,128,1536]{2,1,0:T(8,128)(2,1)S(1)}, bf16[1,128,1536]{2,1,0:T(8,128)(2,1)S(1)}, u32[]{:S(2)}, u32[]{:S(2)}) %collective-permute-start.9) | collective-permute-done | bytes 393248 | tf_op jit(solution)/shard_map/ppermute | solution.py:23
  258.5 7.0 %collective-permute-done.10 = bf16[1,128,1536]{2,1,0:T(8,128)(2,1)S(1)} collective-permute-done((bf16[1,128,1536]{2,1,0:T(8,128)(2,1)S(1)}, bf16[1,128,1536]{2,1,0:T(8,128)(2,1)S(1)}, u32[]{:S(2)}, u32[]{:S(2)}) %collective-permute-start.10) | collective-permute-done | bytes 393248 | tf_op jit(solution)/shard_map/ppermute | solution.py:23
  270.8 5.5 %collective-permute-start.11 = (bf16[1,128,1536]{2,1,0:T(8,128)(2,1)S(1)}, bf16[1,128,1536]{2,1,0:T(8,128)(2,1)S(1)}, u32[]{:S(2)}, u32[]{:S(2)}) collective-permute-start(bf16[1,128,1536]{2,1,0:T(8,128)(2,1)S(1)} %rev.12), channel_id=1, source_target_pairs={{0,32},{1,33},{2,34},{3,35},{4,36},{5,37},{6,38},{7,39},{8,40},{9,... | collective-permute-start | bytes 1179656 | tf_op jit(solution)/shard_map/ppermute | solution.py:17
  279.7 6.2 %collective-permute-done.14 = bf16[1,128,1536]{2,1,0:T(8,128)(2,1)S(1)} collective-permute-done((bf16[1,128,1536]{2,1,0:T(8,128)(2,1)S(1)}, bf16[1,128,1536]{2,1,0:T(8,128)(2,1)S(1)}, u32[]{:S(2)}, u32[]{:S(2)}) %collective-permute-start.14) | collective-permute-done | bytes 393248 | tf_op jit(solution)/shard_map/ppermute | solution.py:17
  288.1 24.9 %collective-permute-done.13 = bf16[1,128,1536]{2,1,0:T(8,128)(2,1)S(1)} collective-permute-done((bf16[1,128,1536]{2,1,0:T(8,128)(2,1)S(1)}, bf16[1,128,1536]{2,1,0:T(8,128)(2,1)S(1)}, u32[]{:S(2)}, u32[]{:S(2)}) %collective-permute-start.13) | collective-permute-done | bytes 393248 | tf_op jit(solution)/shard_map/ppermute | solution.py:17
  332.7 88.4 %psum.7 = f32[1536]{0:T(1024)S(1)} all-reduce(f32[1536]{0:T(1024)S(1)} %get-tuple-element.3), channel_id=1, replica_groups=mesh['dp'=2,'ctx'=128] {'dp','ctx'}, use_global_device_ids=true, to_apply=%region_3.0 | all-reduce | flops 1536 | bytes 12288 | tf_op jit(solution)/shard_map/psum | solution.py:157
  428.5 9.9 %collective-permute-done.17 = bf16[1,128,768]{2,1,0:T(8,128)(2,1)S(1)} collective-permute-done((bf16[1,128,768]{2,1,0:T(8,128)(2,1)S(1)}, bf16[1,128,768]{2,1,0:T(8,128)(2,1)S(1)}, u32[]{:S(2)}, u32[]{:S(2)}) %collective-permute-start.17) | collective-permute-done | bytes 196640 | tf_op jit(solution)/shard_map/ppermute | solution.py:23
  443.1 9.7 %collective-permute-done.18 = bf16[1,128,768]{2,1,0:T(8,128)(2,1)S(1)} collective-permute-done((bf16[1,128,768]{2,1,0:T(8,128)(2,1)S(1)}, bf16[1,128,768]{2,1,0:T(8,128)(2,1)S(1)}, u32[]{:S(2)}, u32[]{:S(2)}) %collective-permute-start.18) | collective-permute-done | bytes 196640 | tf_op jit(solution)/shard_map/ppermute | solution.py:23
  (104 shorter events, 153.2 us)
Async XLA Ops:
  11.4 11.7 %collective-permute-start.28 = (bf16[1,128,768]{2,1,0:T(8,128)(2,1)S(1)}, bf16[1,128,768]{2,1,0:T(8,128)(2,1)S(1)}, u32[]{:S(2)}, u32[]{:S(2)}) collective-permute-start(bf16[1,128,768]{2,1,0:T(8,128)(2,1)S(1)} %collective-permute-done.27), channel_id=1, source_target_pairs={{0,4},{1,5},{2,6},{3,7},{4,0},{5,1},{6,2},{7,3},{8,12},{9,13},{10,... | collective-permute-start | bytes 589832 | tf_op jit(solution)/shard_map/ppermute | solution.py:23
  23.1 12.8 %collective-permute-start.29 = (bf16[1,128,768]{2,1,0:T(8,128)(2,1)S(1)}, bf16[1,128,768]{2,1,0:T(8,128)(2,1)S(1)}, u32[]{:S(2)}, u32[]{:S(2)}) collective-permute-start(bf16[1,128,768]{2,1,0:T(8,128)(2,1)S(1)} %collective-permute-done.28), channel_id=1, source_target_pairs={{0,8},{1,9},{2,10},{3,11},{4,12},{5,13},{6,14},{7,15},{8,0},{9,1},... | collective-permute-start | bytes 589832 | tf_op jit(solution)/shard_map/ppermute | solution.py:23
  53.1 13.2 %collective-permute-start.34 = (bf16[1,128,768]{2,1,0:T(8,128)(2,1)S(1)}, bf16[1,128,768]{2,1,0:T(8,128)(2,1)S(1)}, u32[]{:S(2)}, u32[]{:S(2)}) collective-permute-start(bf16[1,128,768]{2,1,0:T(8,128)(2,1)S(1)} %rev.14), channel_id=1, source_target_pairs={{16,0},{17,1},{18,2},{19,3},{20,4},{21,5},{22,6},{23,7},{24,8},{25... | collective-permute-start | bytes 589832 | tf_op jit(solution)/shard_map/ppermute | solution.py:17
  54.7 20.6 %collective-permute-start.33 = (bf16[1,128,768]{2,1,0:T(8,128)(2,1)S(1)}, bf16[1,128,768]{2,1,0:T(8,128)(2,1)S(1)}, u32[]{:S(2)}, u32[]{:S(2)}) collective-permute-start(bf16[1,128,768]{2,1,0:T(8,128)(2,1)S(1)} %rev.14), channel_id=1, source_target_pairs={{32,0},{33,1},{34,2},{35,3},{36,4},{37,5},{38,6},{39,7},{40,8},{41... | collective-permute-start | bytes 589832 | tf_op jit(solution)/shard_map/ppermute | solution.py:17
  56.3 12.7 %collective-permute-start.35 = (bf16[1,128,768]{2,1,0:T(8,128)(2,1)S(1)}, bf16[1,128,768]{2,1,0:T(8,128)(2,1)S(1)}, u32[]{:S(2)}, u32[]{:S(2)}) collective-permute-start(bf16[1,128,768]{2,1,0:T(8,128)(2,1)S(1)} %rev.14), channel_id=1, source_target_pairs={{0,16},{1,17},{2,18},{3,19},{4,20},{5,21},{6,22},{7,23},{8,24},{9,... | collective-permute-start | bytes 589832 | tf_op jit(solution)/shard_map/ppermute | solution.py:17
  60.3 12.5 %collective-permute-start.36 = (bf16[1,128,768]{2,1,0:T(8,128)(2,1)S(1)}, bf16[1,128,768]{2,1,0:T(8,128)(2,1)S(1)}, u32[]{:S(2)}, u32[]{:S(2)}) collective-permute-start(bf16[1,128,768]{2,1,0:T(8,128)(2,1)S(1)} %rev.14), channel_id=1, source_target_pairs={{0,32},{1,33},{2,34},{3,35},{4,36},{5,37},{6,38},{7,39},{8,40},{9,... | collective-permute-start | bytes 589832 | tf_op jit(solution)/shard_map/ppermute | solution.py:17
  96.3 19.7 %collective-permute-start.39 = (bf16[1,128,1536]{2,1,0:T(8,128)(2,1)S(1)}, bf16[1,128,1536]{2,1,0:T(8,128)(2,1)S(1)}, u32[]{:S(2)}, u32[]{:S(2)}) collective-permute-start(bf16[1,128,1536]{2,1,0:T(8,128)(2,1)S(1)} %collective-permute-done.38), channel_id=1, source_target_pairs={{0,4},{1,5},{2,6},{3,7},{4,0},{5,1},{6,2},{7,3},{8,12},{9,13},{10,... | collective-permute-start | bytes 1179656 | tf_op jit(solution)/shard_map/ppermute | solution.py:23
  116.0 23.2 %collective-permute-start.40 = (bf16[1,128,1536]{2,1,0:T(8,128)(2,1)S(1)}, bf16[1,128,1536]{2,1,0:T(8,128)(2,1)S(1)}, u32[]{:S(2)}, u32[]{:S(2)}) collective-permute-start(bf16[1,128,1536]{2,1,0:T(8,128)(2,1)S(1)} %collective-permute-done.39), channel_id=1, source_target_pairs={{0,8},{1,9},{2,10},{3,11},{4,12},{5,13},{6,14},{7,15},{8,0},{9,1},... | collective-permute-start | bytes 1179656 | tf_op jit(solution)/shard_map/ppermute | solution.py:23
  119.3 33.7 %collective-permute-start.23 = (bf16[1,128,768]{2,1,0:T(8,128)(2,1)S(1)}, bf16[1,128,768]{2,1,0:T(8,128)(2,1)S(1)}, u32[]{:S(2)}, u32[]{:S(2)}) collective-permute-start(bf16[1,128,768]{2,1,0:T(8,128)(2,1)S(1)} %copy-done.2), channel_id=1, source_target_pairs={{16,0},{17,1},{18,2},{19,3},{20,4},{21,5},{22,6},{23,7},{24,8},{25... | collective-permute-start | bytes 589832 | tf_op jit(solution)/shard_map/ppermute | solution.py:17
  120.6 33.3 %collective-permute-start.22 = (bf16[1,128,768]{2,1,0:T(8,128)(2,1)S(1)}, bf16[1,128,768]{2,1,0:T(8,128)(2,1)S(1)}, u32[]{:S(2)}, u32[]{:S(2)}) collective-permute-start(bf16[1,128,768]{2,1,0:T(8,128)(2,1)S(1)} %copy-done.2), channel_id=1, source_target_pairs={{32,0},{33,1},{34,2},{35,3},{36,4},{37,5},{38,6},{39,7},{40,8},{41... | collective-permute-start | bytes 589832 | tf_op jit(solution)/shard_map/ppermute | solution.py:17
  121.9 41.8 %collective-permute-start.25 = (bf16[1,128,768]{2,1,0:T(8,128)(2,1)S(1)}, bf16[1,128,768]{2,1,0:T(8,128)(2,1)S(1)}, u32[]{:S(2)}, u32[]{:S(2)}) collective-permute-start(bf16[1,128,768]{2,1,0:T(8,128)(2,1)S(1)} %copy-done.2), channel_id=1, source_target_pairs={{0,32},{1,33},{2,34},{3,35},{4,36},{5,37},{6,38},{7,39},{8,40},{9,... | collective-permute-start | bytes 589832 | tf_op jit(solution)/shard_map/ppermute | solution.py:17
  130.5 34.1 %collective-permute-start.24 = (bf16[1,128,768]{2,1,0:T(8,128)(2,1)S(1)}, bf16[1,128,768]{2,1,0:T(8,128)(2,1)S(1)}, u32[]{:S(2)}, u32[]{:S(2)}) collective-permute-start(bf16[1,128,768]{2,1,0:T(8,128)(2,1)S(1)} %copy-done.2), channel_id=1, source_target_pairs={{0,16},{1,17},{2,18},{3,19},{4,20},{5,21},{6,22},{7,23},{8,24},{9,... | collective-permute-start | bytes 589832 | tf_op jit(solution)/shard_map/ppermute | solution.py:17
  139.2 12.8 %collective-permute-start.41 = (bf16[1,128,1536]{2,1,0:T(8,128)(2,1)S(1)}, bf16[1,128,1536]{2,1,0:T(8,128)(2,1)S(1)}, u32[]{:S(2)}, u32[]{:S(2)}) collective-permute-start(bf16[1,128,1536]{2,1,0:T(8,128)(2,1)S(1)} %collective-permute-done.40), channel_id=1, source_target_pairs={{0,16},{1,17},{2,18},{3,19},{4,20},{5,21},{6,22},{7,23},{8,24},{9,... | collective-permute-start | bytes 1179656 | tf_op jit(solution)/shard_map/ppermute | solution.py:23
  191.1 20.3 %collective-permute-start.6 = (bf16[1,128,1536]{2,1,0:T(8,128)(2,1)S(1)}, bf16[1,128,1536]{2,1,0:T(8,128)(2,1)S(1)}, u32[]{:S(2)}, u32[]{:S(2)}) collective-permute-start(bf16[1,128,1536]{2,1,0:T(8,128)(2,1)S(1)} %collective-permute-done.5), channel_id=1, source_target_pairs={{0,4},{1,5},{2,6},{3,7},{4,0},{5,1},{6,2},{7,3},{8,12},{9,13},{10,... | collective-permute-start | bytes 1179656 | tf_op jit(solution)/shard_map/ppermute | solution.py:23
  211.5 23.0 %collective-permute-start.7 = (bf16[1,128,1536]{2,1,0:T(8,128)(2,1)S(1)}, bf16[1,128,1536]{2,1,0:T(8,128)(2,1)S(1)}, u32[]{:S(2)}, u32[]{:S(2)}) collective-permute-start(bf16[1,128,1536]{2,1,0:T(8,128)(2,1)S(1)} %collective-permute-done.6), channel_id=1, source_target_pairs={{0,8},{1,9},{2,10},{3,11},{4,12},{5,13},{6,14},{7,15},{8,0},{9,1},... | collective-permute-start | bytes 1179656 | tf_op jit(solution)/shard_map/ppermute | solution.py:23
  269.5 16.5 %collective-permute-start.14 = (bf16[1,128,1536]{2,1,0:T(8,128)(2,1)S(1)}, bf16[1,128,1536]{2,1,0:T(8,128)(2,1)S(1)}, u32[]{:S(2)}, u32[]{:S(2)}) collective-permute-start(bf16[1,128,1536]{2,1,0:T(8,128)(2,1)S(1)} %rev.12), channel_id=1, source_target_pairs={{32,0},{33,1},{34,2},{35,3},{36,4},{37,5},{38,6},{39,7},{40,8},{41... | collective-permute-start | bytes 1179656 | tf_op jit(solution)/shard_map/ppermute | solution.py:17
  270.8 44.3 %collective-permute-start.11 = (bf16[1,128,1536]{2,1,0:T(8,128)(2,1)S(1)}, bf16[1,128,1536]{2,1,0:T(8,128)(2,1)S(1)}, u32[]{:S(2)}, u32[]{:S(2)}) collective-permute-start(bf16[1,128,1536]{2,1,0:T(8,128)(2,1)S(1)} %rev.12), channel_id=1, source_target_pairs={{0,32},{1,33},{2,34},{3,35},{4,36},{5,37},{6,38},{7,39},{8,40},{9,... | collective-permute-start | bytes 1179656 | tf_op jit(solution)/shard_map/ppermute | solution.py:17
  276.3 36.7 %collective-permute-start.13 = (bf16[1,128,1536]{2,1,0:T(8,128)(2,1)S(1)}, bf16[1,128,1536]{2,1,0:T(8,128)(2,1)S(1)}, u32[]{:S(2)}, u32[]{:S(2)}) collective-permute-start(bf16[1,128,1536]{2,1,0:T(8,128)(2,1)S(1)} %rev.12), channel_id=1, source_target_pairs={{16,0},{17,1},{18,2},{19,3},{20,4},{21,5},{22,6},{23,7},{24,8},{25... | collective-permute-start | bytes 1179656 | tf_op jit(solution)/shard_map/ppermute | solution.py:17
  319.4 101.6 %collective-permute-start.15 = (bf16[1,128,768]{2,1,0:T(8,128)(2,1)S(1)}, bf16[1,128,768]{2,1,0:T(8,128)(2,1)S(1)}, u32[]{:S(2)}, u32[]{:S(2)}) collective-permute-start(bf16[1,128,768]{2,1,0:T(8,128)(2,1)S(1)} %fusion.95), channel_id=1, source_target_pairs={{0,1},{1,0},{2,3},{3,2},{4,5},{5,4},{6,7},{7,6},{8,9},{9,8},{10,11... | collective-permute-start | bytes 589832 | tf_op jit(solution)/shard_map/ppermute | solution.py:23
  320.6 120.4 %collective-permute-start.3 = (bf16[1,128,1536]{2,1,0:T(8,128)(2,1)S(1)}, bf16[1,128,1536]{2,1,0:T(8,128)(2,1)S(1)}, u32[]{:S(2)}, u32[]{:S(2)}) collective-permute-start(bf16[1,128,1536]{2,1,0:T(8,128)(2,1)S(1)} %get-tuple-element.7), channel_id=1, source_target_pairs={{32,0},{33,1},{34,2},{35,3},{36,4},{37,5},{38,6},{39,7},{40,8},{41... | collective-permute-start | bytes 1179656 | tf_op jit(solution)/shard_map/ppermute | solution.py:17
  321.9 131.0 %collective-permute-start.2 = (bf16[1,128,1536]{2,1,0:T(8,128)(2,1)S(1)}, bf16[1,128,1536]{2,1,0:T(8,128)(2,1)S(1)}, u32[]{:S(2)}, u32[]{:S(2)}) collective-permute-start(bf16[1,128,1536]{2,1,0:T(8,128)(2,1)S(1)} %get-tuple-element.7), channel_id=1, source_target_pairs={{16,0},{17,1},{18,2},{19,3},{20,4},{21,5},{22,6},{23,7},{24,8},{25... | collective-permute-start | bytes 1179656 | tf_op jit(solution)/shard_map/ppermute | solution.py:17
  323.2 137.1 %collective-permute-start.1 = (bf16[1,128,1536]{2,1,0:T(8,128)(2,1)S(1)}, bf16[1,128,1536]{2,1,0:T(8,128)(2,1)S(1)}, u32[]{:S(2)}, u32[]{:S(2)}) collective-permute-start(bf16[1,128,1536]{2,1,0:T(8,128)(2,1)S(1)} %get-tuple-element.7), channel_id=1, source_target_pairs={{0,16},{1,17},{2,18},{3,19},{4,20},{5,21},{6,22},{7,23},{8,24},{9,... | collective-permute-start | bytes 1179656 | tf_op jit(solution)/shard_map/ppermute | solution.py:17
  327.2 139.5 %collective-permute-start = (bf16[1,128,1536]{2,1,0:T(8,128)(2,1)S(1)}, bf16[1,128,1536]{2,1,0:T(8,128)(2,1)S(1)}, u32[]{:S(2)}, u32[]{:S(2)}) collective-permute-start(bf16[1,128,1536]{2,1,0:T(8,128)(2,1)S(1)} %get-tuple-element.7), channel_id=1, source_target_pairs={{0,32},{1,33},{2,34},{3,35},{4,36},{5,37},{6,38},{7,39},{8,40},{9,... | collective-permute-start | bytes 1179656 | tf_op jit(solution)/shard_map/ppermute | solution.py:17
  438.3 14.5 %collective-permute-start.18 = (bf16[1,128,768]{2,1,0:T(8,128)(2,1)S(1)}, bf16[1,128,768]{2,1,0:T(8,128)(2,1)S(1)}, u32[]{:S(2)}, u32[]{:S(2)}) collective-permute-start(bf16[1,128,768]{2,1,0:T(8,128)(2,1)S(1)} %collective-permute-done.17), channel_id=1, source_target_pairs={{0,8},{1,9},{2,10},{3,11},{4,12},{5,13},{6,14},{7,15},{8,0},{9,1},... | collective-permute-start | bytes 589832 | tf_op jit(solution)/shard_map/ppermute | solution.py:23
  (24 other events, 540.3 us)
where the time goes:
time: 475 us; the launch traced here: 473 us
  waiting for transfers between devices  232 us (49%)
  starting transfers between devices  106 us (22%)
  blocking collectives  88.4 us (19%)
  matrix products  37.1 us (8%)
    ppermute x28, waiting for transfers between devices, partner(): return lax.ppermute(value, axis, pairs)  200 us
    psum x1, blocking collectives, per_device(): summed = lax.psum(partial_sum, ('dp', 'ctx'))  88.4 us
    ppermute x28, starting transfers between devices, partner(): return lax.ppermute(value, axis, pairs)  56.1 us
    ppermute x16, starting transfers between devices, shifted(): return lax.ppermute(block, axis, route)  50.3 us
    ppermute x16, waiting for transfers between devices, shifted(): return lax.ppermute(block, axis, route)  32.3 us
    dot_general x10, matrix products, apply_forward(): jnp.dot(flat_rows, weight[tap_index], preferred_element_type=jnp.float32)  21.5 us
    dot_general x10, matrix products, apply_backward(): lax.dot_general(flat_rows, weight[tap_index], (((1,), (1,)), ((), ())), p...  15.6 us
  transfers between devices with their start and end apart: 44, of which 30 were waited for; matrix products, arithmetic and copies ran while one was open for 6% of the time, Pallas kernels for 0%

commit v1 on v0

v1 whole, which is shorter than its diff:
```python
import math

import jax
import jax.numpy as jnp
from jax import lax
from jax.experimental import pallas as pl
from jax.experimental.pallas import tpu as pltpu
from jax.sharding import PartitionSpec as P

TAPS = 5
EPS = 1e-06
ROWS = 128
CH = 1536
COUT = 768
PART = 512
PARTS = CH // PART
TILE = 256
ROOT = math.sqrt(2.0 / math.pi)
CUBE = 0.044715
BF = jnp.bfloat16
F32 = jnp.float32


def exchange_matrix():
    rows = lax.broadcasted_iota(jnp.int32, (TILE, TILE), 0)
    cols = lax.broadcasted_iota(jnp.int32, (TILE, TILE), 1)
    return jnp.where(rows + cols == TILE - 1, 1.0, 0.0).astype(BF)


def flip_tile(ref, tile, count, swap, rows=slice(None)):
    first = (count - 1 - tile) * TILE
    return jnp.dot(ref[rows, first : first + TILE], swap, preferred_element_type=F32)


def fetch(weight, taps, buffer, sems):
    copies = []
    for slot, tap in enumerate(taps):
        for part in range(PARTS):
            rows = pl.ds(part * PART, PART)
            copy = pltpu.make_async_copy(
                weight.at[tap, rows], buffer.at[slot, rows], sems.at[slot, part]
            )
            copy.start()
            copies.append(copy)
    return copies


def partial_sums(stacked, buffer, sums, copies, count):
    for slot in range(count):
        for part in range(PARTS):
            copies[slot * PARTS + part].wait()
            span = slice(part * PART, (part + 1) * PART)
            term = jnp.dot(stacked[:, span], buffer[slot, span], preferred_element_type=F32)
            if part == 0:
                sums[slot] = term
            else:
                sums[slot] = sums[slot] + term


def forward_far_kernel(place, features, gain, weight, stacked, slope, inv_rms, to_a, to_b, buffer, sums, turned, sems):
    copies = fetch(weight, (0, 4), buffer, sems)
    wide = features[...].astype(F32)
    scale = lax.rsqrt(jnp.mean(wide * wide, axis=-1, keepdims=True) + EPS)
    inv_rms[...] = scale
    swap = exchange_matrix()
    scaled = wide * scale * gain[...]
    square = scaled * scaled
    bend = jnp.tanh(ROOT * (scaled + CUBE * (square * scaled)))
    stacked[:ROWS] = (0.5 * scaled * (1.0 + bend)).astype(BF)
    slope[...] = 0.5 * (1.0 + bend) + 0.5 * scaled * (1.0 - bend * bend) * (
        ROOT * (1.0 + 3.0 * CUBE * square)
    )
    for tile in range(CH // TILE):
        span = slice(tile * TILE, (tile + 1) * TILE)
        stacked[ROWS:, span] = flip_tile(stacked, tile, CH // TILE, swap, slice(0, ROWS)).astype(BF)
    partial_sums(stacked, buffer, sums, copies, 2)
    spot = place[0]
    even = lax.rem(spot, 2) == 0
    turned[...] = sums[:, ROWS:].astype(BF)
    ahead_ok = spot + 2 < 8
    behind_ok = spot - 2 >= 0
    for tile in range(COUT // TILE):
        span = slice(tile * TILE, (tile + 1) * TILE)
        ahead = sums[0, :ROWS, span] + flip_tile(turned.at[1], tile, COUT // TILE, swap)
        behind = sums[1, :ROWS, span] + flip_tile(turned.at[0], tile, COUT // TILE, swap)
        ahead = jnp.where(ahead_ok, ahead, 0.0).astype(BF)
        behind = jnp.where(behind_ok, behind, 0.0).astype(BF)

        @pl.when(even)
        def _(ahead=ahead, behind=behind, span=span):
            to_a[:, span] = ahead
            to_b[:, span] = behind

        @pl.when(jnp.logical_not(even))
        def _(ahead=ahead, behind=behind, span=span):
            to_a[:, span] = behind
            to_b[:, span] = ahead


def forward_near_kernel(place, stacked, from_a, from_b, weight, to_a, to_b, own, buffer, sums, turned, sems):
    copies = fetch(weight, (1, 3, 2), buffer, sems)
    swap = exchange_matrix()
    partial_sums(stacked, buffer, sums, copies, 3)
    spot = place[0]
    even = lax.rem(spot, 2) == 0
    turned[...] = sums[:, ROWS:].astype(BF)
    ahead_ok = spot + 1 < 8
    behind_ok = spot - 1 >= 0
    for tile in range(COUT // TILE):
        span = slice(tile * TILE, (tile + 1) * TILE)
        ahead = sums[0, :ROWS, span] + flip_tile(turned.at[1], tile, COUT // TILE, swap)
        behind = sums[1, :ROWS, span] + flip_tile(turned.at[0], tile, COUT // TILE, swap)
        ahead = jnp.where(ahead_ok, ahead, 0.0)
        behind = jnp.where(behind_ok, behind, 0.0)
        own[:, span] = sums[2, :ROWS, span] + flip_tile(turned.at[2], tile, COUT // TILE, swap)

        @pl.when(even)
        def _(ahead=ahead, behind=behind, span=span):
            to_a[:, span] = (ahead + from_b[:, span].astype(F32)).astype(BF)
            to_b[:, span] = (behind + from_a[:, span].astype(F32)).astype(BF)

        @pl.when(jnp.logical_not(even))
        def _(ahead=ahead, behind=behind, span=span):
            to_a[:, span] = (behind + from_b[:, span].astype(F32)).astype(BF)
            to_b[:, span] = (ahead + from_a[:, span].astype(F32)).astype(BF)


def join_kernel(own, from_a, from_b, convolved):
    convolved[...] = (own[...] + (from_a[...].astype(F32) + from_b[...].astype(F32))).astype(BF)


def stack_pair(lhs, even, ok_ahead, ok_behind, first, second, tap_low, tap_high, swap):
    zero = jnp.zeros((ROWS, COUT), BF)
    for flag, ahead_ref, behind_ref in ((True, first, second), (False, second, first)):

        @pl.when(even if flag else jnp.logical_not(even))
        def _(ahead_ref=ahead_ref, behind_ref=behind_ref):
            lhs[tap_low, :ROWS] = jnp.where(ok_ahead, ahead_ref[...], zero)
            lhs[tap_high, :ROWS] = jnp.where(ok_behind, behind_ref[...], zero)

    for tile in range(COUT // TILE):
        span = slice(tile * TILE, (tile + 1) * TILE)
        lhs[tap_low, ROWS:, span] = flip_tile(lhs.at[tap_high], tile, COUT // TILE, swap, slice(0, ROWS)).astype(BF)
        lhs[tap_high, ROWS:, span] = flip_tile(lhs.at[tap_low], tile, COUT // TILE, swap, slice(0, ROWS)).astype(BF)


def pull_back(lhs, buffer, total, copies, count, fresh):
    for slot in range(count):
        for part in range(PARTS):
            copies[slot * PARTS + part].wait()
            span = slice(part * PART, (part + 1) * PART)
            term = lax.dot_general(
                lhs[slot],
                buffer[slot, span],
                (((1,), (1,)), ((), ())),
                preferred_element_type=F32,
            )
            if slot == 0 and fresh:
                total[:, span] = term
            else:
                total[:, span] = total[:, span] + term


def backward_near_kernel(place, own, from_a, from_b, weight, total, buffer, lhs, sems):
    copies = fetch(weight, (2, 1, 3), buffer, sems)
    swap = exchange_matrix()
    spot = place[0]
    even = lax.rem(spot, 2) == 0
    lhs[0, :ROWS] = own[...]
    for tile in range(COUT // TILE):
        span = slice(tile * TILE, (tile + 1) * TILE)
        lhs[0, ROWS:, span] = flip_tile(own, tile, COUT // TILE, swap).astype(BF)
    stack_pair(lhs, even, spot + 1 < 8, spot - 1 >= 0, from_a, from_b, 1, 2, swap)
    pull_back(lhs, buffer, total, copies, 3, True)


def backward_far_kernel(
    place, from_a, from_b, weight, near, features, gain, slope, inv_rms, grad, gain_part, total, buffer, lhs, turned, sems
):
    copies = fetch(weight, (0, 4), buffer, sems)
    swap = exchange_matrix()
    spot = place[0]
    even = lax.rem(spot, 2) == 0
    stack_pair(lhs, even, spot + 2 < 8, spot - 2 >= 0, from_a, from_b, 0, 1, swap)
    total[...] = near[...]
    pull_back(lhs, buffer, total, copies, 2, False)
    turned[...] = total[ROWS:].astype(BF)
    scale = inv_rms[...]
    spread = jnp.zeros((ROWS, 1), F32)
    for tile in range(CH // TILE):
        span = slice(tile * TILE, (tile + 1) * TILE)
        hidden_grad = total[:ROWS, span] + flip_tile(turned, tile, CH // TILE, swap)
        scaled_grad = hidden_grad * slope[:, span]
        product = scaled_grad * (features[:, span].astype(F32) * scale)
        gain_part[:, span] = jnp.sum(product, axis=0, keepdims=True)
        spread = spread + jnp.sum(product * gain[:, span], axis=-1, keepdims=True)
        total[:ROWS, span] = scaled_grad * gain[:, span]
    spread = spread * (1.0 / CH)
    normed = features[...].astype(F32) * scale
    grad[...] = (scale * (total[:ROWS] - normed * spread)).astype(BF)


VMEM = pl.BlockSpec(memory_space=pltpu.VMEM)
SMEM = pl.BlockSpec(memory_space=pltpu.SMEM)
HBM = pl.BlockSpec(memory_space=pl.ANY)
LIMIT = pltpu.CompilerParams(vmem_limit_bytes=56 * 2**20)


def shape(dims, kind):
    return jax.ShapeDtypeStruct(dims, kind)


def forward_far(place, features, gain, weight):
    return pl.pallas_call(
        forward_far_kernel,
        out_shape=(
            shape((2 * ROWS, CH), BF),
            shape((ROWS, CH), F32),
            shape((ROWS, 1), F32),
            shape((ROWS, COUT), BF),
            shape((ROWS, COUT), BF),
        ),
        in_specs=[SMEM, VMEM, VMEM, HBM],
        out_specs=[VMEM] * 5,
        scratch_shapes=[
            pltpu.VMEM((2, CH, COUT), BF),
            pltpu.VMEM((2, 2 * ROWS, COUT), F32),
            pltpu.VMEM((2, ROWS, COUT), BF),
            pltpu.SemaphoreType.DMA((2, PARTS)),
        ],
        compiler_params=LIMIT,
        cost_estimate=pl.CostEstimate(flops=1300000000, bytes_accessed=7000000, transcendentals=200000),
        name="forward_far",
    )(place, features, gain, weight)


def forward_near(place, stacked, from_a, from_b, weight):
    return pl.pallas_call(
        forward_near_kernel,
        out_shape=(
            shape((ROWS, COUT), BF),
            shape((ROWS, COUT), BF),
            shape((ROWS, COUT), F32),
        ),
        in_specs=[SMEM, VMEM, VMEM, VMEM, HBM],
        out_specs=[VMEM] * 3,
        scratch_shapes=[
            pltpu.VMEM((3, CH, COUT), BF),
            pltpu.VMEM((3, 2 * ROWS, COUT), F32),
            pltpu.VMEM((3, ROWS, COUT), BF),
            pltpu.SemaphoreType.DMA((3, PARTS)),
        ],
        compiler_params=LIMIT,
        cost_estimate=pl.CostEstimate(flops=1900000000, bytes_accessed=9000000, transcendentals=0),
        name="forward_near",
    )(place, stacked, from_a, from_b, weight)


def join(own, from_a, from_b):
    return pl.pallas_call(
        join_kernel,
        out_shape=shape((ROWS, COUT), BF),
        in_specs=[VMEM] * 3,
        out_specs=VMEM,
        cost_estimate=pl.CostEstimate(flops=200000, bytes_accessed=1000000, transcendentals=0),
        name="join",
    )(own, from_a, from_b)


def backward_near(place, own, from_a, from_b, weight):
    return pl.pallas_call(
        backward_near_kernel,
        out_shape=shape((2 * ROWS, CH), F32),
        in_specs=[SMEM, VMEM, VMEM, VMEM, HBM],
        out_specs=VMEM,
        scratch_shapes=[
            pltpu.VMEM((3, CH, COUT), BF),
            pltpu.VMEM((3, 2 * ROWS, COUT), BF),
            pltpu.SemaphoreType.DMA((3, PARTS)),
        ],
        compiler_params=LIMIT,
        cost_estimate=pl.CostEstimate(flops=1900000000, bytes_accessed=9000000, transcendentals=0),
        name="backward_near",
    )(place, own, from_a, from_b, weight)


def backward_far(place, from_a, from_b, weight, near, features, gain, slope, inv_rms):
    return pl.pallas_call(
        backward_far_kernel,
        out_shape=(shape((ROWS, CH), BF), shape((1, CH), F32)),
        in_specs=[SMEM, VMEM, VMEM, HBM, VMEM, VMEM, VMEM, VMEM, VMEM],
        out_specs=[VMEM] * 2,
        scratch_shapes=[
            pltpu.VMEM((2 * ROWS, CH), F32),
            pltpu.VMEM((2, CH, COUT), BF),
            pltpu.VMEM((2, 2 * ROWS, COUT), BF),
            pltpu.VMEM((ROWS, CH), BF),
            pltpu.SemaphoreType.DMA((2, PARTS)),
        ],
        compiler_params=LIMIT,
        cost_estimate=pl.CostEstimate(flops=1300000000, bytes_accessed=7000000, transcendentals=0),
        name="backward_far",
    )(place, from_a, from_b, weight, near, features, gain, slope, inv_rms)


def exchange_a(value):
    return lax.ppermute(value, "ctx", [(i, ((i // 16) ^ 1) * 16 + i % 16) for i in range(128)])


def exchange_b(value):
    pairs = []
    for i in range(128):
        spot = i // 16
        other = (spot + 1) % 8 if spot % 2 else (spot - 1) % 8
        pairs.append((i, other * 16 + i % 16))
    return lax.ppermute(value, "ctx", pairs)


BOTH = ("dp", "ctx")


def turn(value, base, radix, step):
    pairs = []
    for i in range(256):
        digit = (i // base) % radix
        pairs.append((i, i + ((digit + step) % radix - digit) * base))
    return lax.ppermute(value, BOTH, pairs)


def sum_everywhere(value):
    for base, radix in ((1, 4), (4, 4), (16, 4), (64, 4)):
        others = [turn(value, base, radix, step) for step in range(1, radix)]
        for other in others:
            value = value + other
    return value


def per_device(features, gain, conv_weight, cotangent):
    spot = (lax.axis_index("ctx") // 16).astype(jnp.int32)
    place = spot.reshape(1)
    rows = features.reshape(ROWS, CH)
    gain_row = gain.reshape(1, CH)
    own = cotangent.reshape(ROWS, COUT)
    grad_a = exchange_a(own)
    grad_b = exchange_b(own)
    stacked, slope, inv_rms, to_a, to_b = forward_far(place, rows, gain_row, conv_weight)
    grad_ba = exchange_a(grad_b)
    grad_ab = exchange_b(grad_a)
    near = backward_near(place, own, grad_a, grad_b, conv_weight)
    input_grad, gain_part = backward_far(
        place, grad_ba, grad_ab, conv_weight, near, rows, gain_row, slope, inv_rms
    )
    far_a = exchange_a(to_a)
    far_b = exchange_b(to_b)
    near_a, near_b, own_term = forward_near(place, stacked, far_a, far_b, conv_weight)
    convolved = join(own_term, exchange_a(near_a), exchange_b(near_b))
    summed = sum_everywhere(gain_part)
    total_rows = 2 * 16384
    gain_grad = summed.reshape(CH) / math.sqrt(total_rows)
    return (
        convolved.reshape(1, ROWS, COUT),
        input_grad.reshape(1, ROWS, CH),
        gain_grad,
    )


def solution(mesh):
    return jax.shard_map(
        per_device,
        mesh=mesh,
        in_specs=(P("dp", "ctx", None), P(), P(), P("dp", "ctx", None)),
        out_specs=(P("dp", "ctx", None), P("dp", "ctx", None), P()),
        check_vma=False,
    )
```

time: 475 us -> 83.6 us (0.18)
  the two profiles are of different devices: /device:TPU:1 before, /device:TPU:64 now
where the time goes in v1:
time: 83.6 us; the launch traced here: 83.3 us
  starting transfers between devices  33.1 us (40%)
  Pallas kernels  29.9 us (36%)
  waiting for transfers between devices  14.8 us (18%)
  local copies, waits for them, and re-layouts  3.4 us (4%)
  other arithmetic  1.36 us (2%)
    ppermute x12, starting transfers between devices, turn(): return lax.ppermute(value, BOTH, pairs)  19.3 us
    ppermute x4, starting transfers between devices, exchange_b(): return lax.ppermute(value, 'ctx', pairs)  13.7 us
    ppermute x4, waiting for transfers between devices, exchange_b(): return lax.ppermute(value, 'ctx', pairs)  10.1 us
    pallas_call x1, Pallas kernels, forward_near(): pl.pallas_call(forward_near_kernel, out_shape=(shape((ROWS, COUT), BF), s...  8.18 us
    pallas_call x1, Pallas kernels, forward_far(): pl.pallas_call(forward_far_kernel, out_shape=(shape((2 * ROWS, CH), BF),...  6.89 us
    pallas_call x1, Pallas kernels, backward_near(): pl.pallas_call(backward_near_kernel, out_shape=shape((2 * ROWS, CH), F32)...  6.53 us
    pallas_call x1, Pallas kernels, backward_far(): pl.pallas_call(backward_far_kernel, out_shape=(shape((ROWS, CH), BF), sha...  6.42 us
    ppermute x12, waiting for transfers between devices, turn(): return lax.ppermute(value, BOTH, pairs)  3.14 us
  transfers between devices with their start and end apart: 20, of which 7 were waited for; matrix products, arithmetic and copies ran while one was open for 2% of the time, Pallas kernels for 28%

profile of v1, /device:TPU:64, one launch (start us, length us, event | category | flops | bytes accessed | tf_op | source)
XLA Modules:
  0.0 83.3 jit_solution(2883445063969258063)
XLA Ops:
  0.6 5.6 %collective-permute-start.4 = (bf16[128,768]{1,0:T(8,128)(2,1)}, bf16[128,768]{1,0:T(8,128)(2,1)S(1)}, u32[]{:S(2)}, u32[]{:S(2)}) collective-permute-start(bf16[128,768]{1,0:T(8,128)(2,1)} %bitcast.8), channel_id=1, source_target_pairs={{0,112},{1,113},{2,114},{3,115},{4,116},{5,117},{6,118},{7,119},{8... | collective-permute-start | bytes 589832 | tf_op jit(solution)/shard_map/ppermute | solution.py:316
  6.2 1.3 %reshape.29.gain = f32[1,1536]{1,0:T(1,128)} reshape(f32[1536]{0:T(1024)} %param.5) | data formatting | bytes 12288 | tf_op jit(solution)/shard_map/reshape | solution.py:342
  7.5 3.8 %collective-permute-done.4.from_b = bf16[128,768]{1,0:T(8,128)(2,1)S(1)} collective-permute-done((bf16[128,768]{1,0:T(8,128)(2,1)}, bf16[128,768]{1,0:T(8,128)(2,1)S(1)}, u32[]{:S(2)}, u32[]{:S(2)}) %collective-permute-start.4) | collective-permute-done | bytes 196640 | tf_op jit(solution)/shard_map/ppermute | solution.py:316
  11.3 1.5 %collective-permute-done.6.from_a = bf16[128,768]{1,0:T(8,128)(2,1)S(1)} collective-permute-done((bf16[128,768]{1,0:T(8,128)(2,1)}, bf16[128,768]{1,0:T(8,128)(2,1)S(1)}, u32[]{:S(2)}, u32[]{:S(2)}) %collective-permute-start.6) | collective-permute-done | bytes 196640 | tf_op jit(solution)/shard_map/ppermute | solution.py:307
  12.8 4.0 %collective-permute-start.7 = (bf16[128,768]{1,0:T(8,128)(2,1)S(1)}, bf16[128,768]{1,0:T(8,128)(2,1)S(1)}, u32[]{:S(2)}, u32[]{:S(2)}) collective-permute-start(bf16[128,768]{1,0:T(8,128)(2,1)S(1)} %collective-permute-done.6.from_a), channel_id=1, source_target_pairs={{0,112},{1,113},{2,114},{3,115},{4,116},{5,117},{6,118},{7,119},{8... | collective-permute-start | bytes 589832 | tf_op jit(solution)/shard_map/ppermute | solution.py:316
  16.8 6.9 %forward_far.1 = (bf16[256,1536]{1,0:T(8,128)(2,1)}, f32[128,1536]{1,0:T(8,128)}, f32[128,1]{1,0:T(8,128)}, bf16[128,768]{1,0:T(8,128)(2,1)}, bf16[128,768]{1,0:T(8,128)(2,1)}) custom-call(s32[1]{0:T(128)} %bitcast.place, bf16[128,1536]{1,0:T(8,128)(2,1)} %bitcast.5, f32[1,1536]{1,0:T(1,128)} %reshape.29.gain, bf16[5,1536,768]{2,1,0:T(8,128)(2,1)} %weight.7), custom_call_target="tpu_custom_call" | custom-call | flops 1300000000 | bytes 7000000 | tf_op jit(solution)/shard_map/forward_far/pallas_call | solution.py:214
  23.7 6.5 %backward_near.1.near = f32[256,1536]{1,0:T(8,128)} custom-call(s32[1]{0:T(128)} %bitcast.place, bf16[128,768]{1,0:T(8,128)(2,1)} %bitcast.10, bf16[128,768]{1,0:T(8,128)(2,1)} %copy-done.5, bf16[128,768]{1,0:T(8,128)(2,1)} %copy-done.4, bf16[5,1536,768]{2,1,0:T(8,128)(2,1)} %weight.7), custom_call_target="tpu_custom_call" | custom-call | flops 1900000000 | bytes 9000000 | tf_op jit(solution)/shard_map/backward_near/pallas_call | solution.py:271
  31.0 6.4 %backward_far.1 = (bf16[128,1536]{1,0:T(8,128)(2,1)}, f32[1,1536]{1,0:T(1,128)}) custom-call(s32[1]{0:T(128)} %bitcast.place, bf16[128,768]{1,0:T(8,128)(2,1)} %copy-done, bf16[128,768]{1,0:T(8,128)(2,1)} %copy-done.1, bf16[5,1536,768]{2,1,0:T(8,128)(2,1)} %weight.7, f32[256,1536]{1,0:T(8,128)} %backward_near.1.near, bf16[128,1536]{1,0:T(8,128)(2,1)} %bitcast.6, ...), custom_call_target="tpu_custom_call" | custom-call | flops 1300000000 | bytes 7000000 | tf_op jit(solution)/shard_map/backward_far/pallas_call | solution.py:288
  37.7 1.8 %collective-permute-start.9 = (f32[1,1536]{1,0:T(1,128)}, f32[1,1536]{1,0:T(1,128)S(1)}, u32[]{:S(2)}, u32[]{:S(2)}) collective-permute-start(f32[1,1536]{1,0:T(1,128)} %get-tuple-element.22), channel_id=1, source_target_pairs={{0,2},{1,3},{2,0},{3,1},{4,6},{5,7},{6,4},{7,5},{8,10},{9,11},{10,... | collective-permute-start | bytes 18440 | tf_op jit(solution)/shard_map/ppermute | solution.py:327
  39.7 1.9 %collective-permute-done.9 = f32[1,1536]{1,0:T(1,128)S(1)} collective-permute-done((f32[1,1536]{1,0:T(1,128)}, f32[1,1536]{1,0:T(1,128)S(1)}, u32[]{:S(2)}, u32[]{:S(2)}) %collective-permute-start.9) | collective-permute-done | bytes 6176 | tf_op jit(solution)/shard_map/ppermute | solution.py:327
  41.6 1.2 %collective-permute-done.8 = f32[1,1536]{1,0:T(1,128)S(1)} collective-permute-done((f32[1,1536]{1,0:T(1,128)}, f32[1,1536]{1,0:T(1,128)S(1)}, u32[]{:S(2)}, u32[]{:S(2)}) %collective-permute-start.8) | collective-permute-done | bytes 6176 | tf_op jit(solution)/shard_map/ppermute | solution.py:327
  42.8 0.7 add_add_fusion.2
  43.6 5.9 %collective-permute-start.12 = (f32[1,1536]{1,0:T(1,128)S(1)}, f32[1,1536]{1,0:T(1,128)S(1)}, u32[]{:S(2)}, u32[]{:S(2)}) collective-permute-start(f32[1,1536]{1,0:T(1,128)S(1)} %add_add_fusion.2), channel_id=1, source_target_pairs={{0,8},{1,9},{2,10},{3,11},{4,12},{5,13},{6,14},{7,15},{8,0},{9,1},... | collective-permute-start | bytes 18440 | tf_op jit(solution)/shard_map/ppermute | solution.py:327
  49.5 2.7 %collective-permute-start.11 = (f32[1,1536]{1,0:T(1,128)S(1)}, f32[1,1536]{1,0:T(1,128)S(1)}, u32[]{:S(2)}, u32[]{:S(2)}) collective-permute-start(f32[1,1536]{1,0:T(1,128)S(1)} %add_add_fusion.2), channel_id=1, source_target_pairs={{0,4},{1,5},{2,6},{3,7},{4,8},{5,9},{6,10},{7,11},{8,12},{9,13},{1... | collective-permute-start | bytes 18440 | tf_op jit(solution)/shard_map/ppermute | solution.py:327
  52.2 2.0 %collective-permute-start.1 = (bf16[128,768]{1,0:T(8,128)(2,1)S(1)}, bf16[128,768]{1,0:T(8,128)(2,1)S(1)}, u32[]{:S(2)}, u32[]{:S(2)}) collective-permute-start(bf16[128,768]{1,0:T(8,128)(2,1)S(1)} %copy-done.8), channel_id=1, source_target_pairs={{0,112},{1,113},{2,114},{3,115},{4,116},{5,117},{6,118},{7,119},{8... | collective-permute-start | bytes 589832 | tf_op jit(solution)/shard_map/ppermute | solution.py:316
  54.3 2.6 %collective-permute-start.16 = (f32[1,1536]{1,0:T(1,128)S(1)}, f32[1,1536]{1,0:T(1,128)S(1)}, u32[]{:S(2)}, u32[]{:S(2)}) collective-permute-start(f32[1,1536]{1,0:T(1,128)S(1)} %add_add_fusion.1), channel_id=1, source_target_pairs={{0,48},{1,49},{2,50},{3,51},{4,52},{5,53},{6,54},{7,55},{8,56},{9,... | collective-permute-start | bytes 18440 | tf_op jit(solution)/shard_map/ppermute | solution.py:327
  56.9 1.0 %collective-permute-start.14 = (f32[1,1536]{1,0:T(1,128)S(1)}, f32[1,1536]{1,0:T(1,128)S(1)}, u32[]{:S(2)}, u32[]{:S(2)}) collective-permute-start(f32[1,1536]{1,0:T(1,128)S(1)} %add_add_fusion.1), channel_id=1, source_target_pairs={{0,16},{1,17},{2,18},{3,19},{4,20},{5,21},{6,22},{7,23},{8,24},{9,... | collective-permute-start | bytes 18440 | tf_op jit(solution)/shard_map/ppermute | solution.py:327
  57.9 3.6 %collective-permute-done.1.from_b = bf16[128,768]{1,0:T(8,128)(2,1)S(1)} collective-permute-done((bf16[128,768]{1,0:T(8,128)(2,1)S(1)}, bf16[128,768]{1,0:T(8,128)(2,1)S(1)}, u32[]{:S(2)}, u32[]{:S(2)}) %collective-permute-start.1) | collective-permute-done | bytes 196640 | tf_op jit(solution)/shard_map/ppermute | solution.py:316
  62.3 8.2 %forward_near.1 = (bf16[128,768]{1,0:T(8,128)(2,1)}, bf16[128,768]{1,0:T(8,128)(2,1)}, f32[128,768]{1,0:T(8,128)}) custom-call(s32[1]{0:T(128)} %bitcast.place, bf16[256,1536]{1,0:T(8,128)(2,1)} %get-tuple-element.13.stacked, bf16[128,768]{1,0:T(8,128)(2,1)} %copy-done.6, bf16[128,768]{1,0:T(8,128)(2,1)} %copy-done.7, bf16[5,1536,768]{2,1,0:T(8,128)(2,1)} %weight.7), custom_call_target="tpu_custom_call" | custom-call | flops 1900000000 | bytes 9000000 | tf_op jit(solution)/shard_map/forward_near/pallas_call | solution.py:238
  70.6 2.1 %collective-permute-start.3 = (bf16[128,768]{1,0:T(8,128)(2,1)}, bf16[128,768]{1,0:T(8,128)(2,1)S(1)}, u32[]{:S(2)}, u32[]{:S(2)}) collective-permute-start(bf16[128,768]{1,0:T(8,128)(2,1)} %get-tuple-element.18), channel_id=1, source_target_pairs={{0,112},{1,113},{2,114},{3,115},{4,116},{5,117},{6,118},{7,119},{8... | collective-permute-start | bytes 589832 | tf_op jit(solution)/shard_map/ppermute | solution.py:316
  72.7 1.1 %collective-permute-start.19 = (f32[1,1536]{1,0:T(1,128)S(1)}, f32[1,1536]{1,0:T(1,128)S(1)}, u32[]{:S(2)}, u32[]{:S(2)}) collective-permute-start(f32[1,1536]{1,0:T(1,128)S(1)} %add_add_fusion), channel_id=1, source_target_pairs={{0,192},{1,193},{2,194},{3,195},{4,196},{5,197},{6,198},{7,199},{8... | collective-permute-start | bytes 18440 | tf_op jit(solution)/shard_map/ppermute | solution.py:327
  74.0 3.6 %collective-permute-start.17 = (f32[1,1536]{1,0:T(1,128)S(1)}, f32[1,1536]{1,0:T(1,128)S(1)}, u32[]{:S(2)}, u32[]{:S(2)}) collective-permute-start(f32[1,1536]{1,0:T(1,128)S(1)} %add_add_fusion), channel_id=1, source_target_pairs={{0,64},{1,65},{2,66},{3,67},{4,68},{5,69},{6,70},{7,71},{8,72},{9,... | collective-permute-start | bytes 18440 | tf_op jit(solution)/shard_map/ppermute | solution.py:327
  77.5 2.6 %collective-permute-done.3.from_b = bf16[128,768]{1,0:T(8,128)(2,1)S(1)} collective-permute-done((bf16[128,768]{1,0:T(8,128)(2,1)}, bf16[128,768]{1,0:T(8,128)(2,1)S(1)}, u32[]{:S(2)}, u32[]{:S(2)}) %collective-permute-start.3) | collective-permute-done | bytes 196640 | tf_op jit(solution)/shard_map/ppermute | solution.py:316
  80.8 1.9 %join.1 = bf16[128,768]{1,0:T(8,128)(2,1)} custom-call(f32[128,768]{1,0:T(8,128)} %get-tuple-element.16.own, bf16[128,768]{1,0:T(8,128)(2,1)} %copy-done.2, bf16[128,768]{1,0:T(8,128)(2,1)} %copy-done.3), custom_call_target="tpu_custom_call" | custom-call | flops 200000 | bytes 1000000 | tf_op jit(solution)/shard_map/join/pallas_call | solution.py:260
  (46 shorter events, 3.6 us)
Async XLA Ops:
  0.6 10.7 %collective-permute-start.4 = (bf16[128,768]{1,0:T(8,128)(2,1)}, bf16[128,768]{1,0:T(8,128)(2,1)S(1)}, u32[]{:S(2)}, u32[]{:S(2)}) collective-permute-start(bf16[128,768]{1,0:T(8,128)(2,1)} %bitcast.8), channel_id=1, source_target_pairs={{0,112},{1,113},{2,114},{3,115},{4,116},{5,117},{6,118},{7,119},{8... | collective-permute-start | bytes 589832 | tf_op jit(solution)/shard_map/ppermute | solution.py:316
  6.2 6.6 %collective-permute-start.6 = (bf16[128,768]{1,0:T(8,128)(2,1)}, bf16[128,768]{1,0:T(8,128)(2,1)S(1)}, u32[]{:S(2)}, u32[]{:S(2)}) collective-permute-start(bf16[128,768]{1,0:T(8,128)(2,1)} %bitcast.9), channel_id=1, source_target_pairs={{0,16},{1,17},{2,18},{3,19},{4,20},{5,21},{6,22},{7,23},{8,24},{9,... | collective-permute-start | bytes 589832 | tf_op jit(solution)/shard_map/ppermute | solution.py:307
  11.3 12.4 %copy-start.4 = (bf16[128,768]{1,0:T(8,128)(2,1)}, bf16[128,768]{1,0:T(8,128)(2,1)S(1)}, u32[]{:S(2)}) copy-start(bf16[128,768]{1,0:T(8,128)(2,1)S(1)} %collective-permute-done.4.from_b) | copy-start | bytes 589828
  11.3 18.9 %collective-permute-start.5 = (bf16[128,768]{1,0:T(8,128)(2,1)S(1)}, bf16[128,768]{1,0:T(8,128)(2,1)S(1)}, u32[]{:S(2)}, u32[]{:S(2)}) collective-permute-start(bf16[128,768]{1,0:T(8,128)(2,1)S(1)} %collective-permute-done.4.from_b), channel_id=1, source_target_pairs={{0,16},{1,17},{2,18},{3,19},{4,20},{5,21},{6,22},{7,23},{8,24},{9,... | collective-permute-start | bytes 589832 | tf_op jit(solution)/shard_map/ppermute | solution.py:307
  12.8 10.9 %copy-start.5 = (bf16[128,768]{1,0:T(8,128)(2,1)}, bf16[128,768]{1,0:T(8,128)(2,1)S(1)}, u32[]{:S(2)}) copy-start(bf16[128,768]{1,0:T(8,128)(2,1)S(1)} %collective-permute-done.6.from_a) | copy-start | bytes 589828
  12.8 17.5 %collective-permute-start.7 = (bf16[128,768]{1,0:T(8,128)(2,1)S(1)}, bf16[128,768]{1,0:T(8,128)(2,1)S(1)}, u32[]{:S(2)}, u32[]{:S(2)}) collective-permute-start(bf16[128,768]{1,0:T(8,128)(2,1)S(1)} %collective-permute-done.6.from_a), channel_id=1, source_target_pairs={{0,112},{1,113},{2,114},{3,115},{4,116},{5,117},{6,118},{7,119},{8... | collective-permute-start | bytes 589832 | tf_op jit(solution)/shard_map/ppermute | solution.py:316
  23.7 28.5 %copy-start.9 = (bf16[128,768]{1,0:T(8,128)(2,1)S(1)}, bf16[128,768]{1,0:T(8,128)(2,1)}, u32[]{:S(2)}) copy-start(bf16[128,768]{1,0:T(8,128)(2,1)} %get-tuple-element.14) | copy-start | bytes 589828
  23.7 28.5 %copy-start.8 = (bf16[128,768]{1,0:T(8,128)(2,1)S(1)}, bf16[128,768]{1,0:T(8,128)(2,1)}, u32[]{:S(2)}) copy-start(bf16[128,768]{1,0:T(8,128)(2,1)} %get-tuple-element.15) | copy-start | bytes 589828
  37.4 2.2 %collective-permute-start.10 = (f32[1,1536]{1,0:T(1,128)}, f32[1,1536]{1,0:T(1,128)S(1)}, u32[]{:S(2)}, u32[]{:S(2)}) collective-permute-start(f32[1,1536]{1,0:T(1,128)} %get-tuple-element.22), channel_id=1, source_target_pairs={{0,3},{1,0},{2,1},{3,2},{4,7},{5,4},{6,5},{7,6},{8,11},{9,8},{10,9... | collective-permute-start | bytes 18440 | tf_op jit(solution)/shard_map/ppermute | solution.py:327
  37.7 3.8 %collective-permute-start.9 = (f32[1,1536]{1,0:T(1,128)}, f32[1,1536]{1,0:T(1,128)S(1)}, u32[]{:S(2)}, u32[]{:S(2)}) collective-permute-start(f32[1,1536]{1,0:T(1,128)} %get-tuple-element.22), channel_id=1, source_target_pairs={{0,2},{1,3},{2,0},{3,1},{4,6},{5,7},{6,4},{7,5},{8,10},{9,11},{10,... | collective-permute-start | bytes 18440 | tf_op jit(solution)/shard_map/ppermute | solution.py:327
  39.5 3.3 %collective-permute-start.8 = (f32[1,1536]{1,0:T(1,128)}, f32[1,1536]{1,0:T(1,128)S(1)}, u32[]{:S(2)}, u32[]{:S(2)}) collective-permute-start(f32[1,1536]{1,0:T(1,128)} %get-tuple-element.22), channel_id=1, source_target_pairs={{0,1},{1,2},{2,3},{3,0},{4,5},{5,6},{6,7},{7,4},{8,9},{9,10},{10,1... | collective-permute-start | bytes 18440 | tf_op jit(solution)/shard_map/ppermute | solution.py:327
  43.5 10.7 %collective-permute-start.13 = (f32[1,1536]{1,0:T(1,128)S(1)}, f32[1,1536]{1,0:T(1,128)S(1)}, u32[]{:S(2)}, u32[]{:S(2)}) collective-permute-start(f32[1,1536]{1,0:T(1,128)S(1)} %add_add_fusion.2), channel_id=1, source_target_pairs={{0,12},{1,13},{2,14},{3,15},{4,0},{5,1},{6,2},{7,3},{8,4},{9,5},{1... | collective-permute-start | bytes 18440 | tf_op jit(solution)/shard_map/ppermute | solution.py:327
  43.6 10.6 %collective-permute-start.12 = (f32[1,1536]{1,0:T(1,128)S(1)}, f32[1,1536]{1,0:T(1,128)S(1)}, u32[]{:S(2)}, u32[]{:S(2)}) collective-permute-start(f32[1,1536]{1,0:T(1,128)S(1)} %add_add_fusion.2), channel_id=1, source_target_pairs={{0,8},{1,9},{2,10},{3,11},{4,12},{5,13},{6,14},{7,15},{8,0},{9,1},... | collective-permute-start | bytes 18440 | tf_op jit(solution)/shard_map/ppermute | solution.py:327
  49.5 4.7 %collective-permute-start.11 = (f32[1,1536]{1,0:T(1,128)S(1)}, f32[1,1536]{1,0:T(1,128)S(1)}, u32[]{:S(2)}, u32[]{:S(2)}) collective-permute-start(f32[1,1536]{1,0:T(1,128)S(1)} %add_add_fusion.2), channel_id=1, source_target_pairs={{0,4},{1,5},{2,6},{3,7},{4,8},{5,9},{6,10},{7,11},{8,12},{9,13},{1... | collective-permute-start | bytes 18440 | tf_op jit(solution)/shard_map/ppermute | solution.py:327
  52.2 5.7 %collective-permute-start = (bf16[128,768]{1,0:T(8,128)(2,1)S(1)}, bf16[128,768]{1,0:T(8,128)(2,1)S(1)}, u32[]{:S(2)}, u32[]{:S(2)}) collective-permute-start(bf16[128,768]{1,0:T(8,128)(2,1)S(1)} %copy-done.9), channel_id=1, source_target_pairs={{0,16},{1,17},{2,18},{3,19},{4,20},{5,21},{6,22},{7,23},{8,24},{9,... | collective-permute-start | bytes 589832 | tf_op jit(solution)/shard_map/ppermute | solution.py:307
  52.2 9.4 %collective-permute-start.1 = (bf16[128,768]{1,0:T(8,128)(2,1)S(1)}, bf16[128,768]{1,0:T(8,128)(2,1)S(1)}, u32[]{:S(2)}, u32[]{:S(2)}) collective-permute-start(bf16[128,768]{1,0:T(8,128)(2,1)S(1)} %copy-done.8), channel_id=1, source_target_pairs={{0,112},{1,113},{2,114},{3,115},{4,116},{5,117},{6,118},{7,119},{8... | collective-permute-start | bytes 589832 | tf_op jit(solution)/shard_map/ppermute | solution.py:316
  54.3 18.4 %collective-permute-start.16 = (f32[1,1536]{1,0:T(1,128)S(1)}, f32[1,1536]{1,0:T(1,128)S(1)}, u32[]{:S(2)}, u32[]{:S(2)}) collective-permute-start(f32[1,1536]{1,0:T(1,128)S(1)} %add_add_fusion.1), channel_id=1, source_target_pairs={{0,48},{1,49},{2,50},{3,51},{4,52},{5,53},{6,54},{7,55},{8,56},{9,... | collective-permute-start | bytes 18440 | tf_op jit(solution)/shard_map/ppermute | solution.py:327
  56.9 15.8 %collective-permute-start.15 = (f32[1,1536]{1,0:T(1,128)S(1)}, f32[1,1536]{1,0:T(1,128)S(1)}, u32[]{:S(2)}, u32[]{:S(2)}) collective-permute-start(f32[1,1536]{1,0:T(1,128)S(1)} %add_add_fusion.1), channel_id=1, source_target_pairs={{0,32},{1,33},{2,34},{3,35},{4,36},{5,37},{6,38},{7,39},{8,40},{9,... | collective-permute-start | bytes 18440 | tf_op jit(solution)/shard_map/ppermute | solution.py:327
  56.9 15.8 %collective-permute-start.14 = (f32[1,1536]{1,0:T(1,128)S(1)}, f32[1,1536]{1,0:T(1,128)S(1)}, u32[]{:S(2)}, u32[]{:S(2)}) collective-permute-start(f32[1,1536]{1,0:T(1,128)S(1)} %add_add_fusion.1), channel_id=1, source_target_pairs={{0,16},{1,17},{2,18},{3,19},{4,20},{5,21},{6,22},{7,23},{8,24},{9,... | collective-permute-start | bytes 18440 | tf_op jit(solution)/shard_map/ppermute | solution.py:327
  70.5 7.1 %collective-permute-start.2 = (bf16[128,768]{1,0:T(8,128)(2,1)}, bf16[128,768]{1,0:T(8,128)(2,1)S(1)}, u32[]{:S(2)}, u32[]{:S(2)}) collective-permute-start(bf16[128,768]{1,0:T(8,128)(2,1)} %get-tuple-element.17), channel_id=1, source_target_pairs={{0,16},{1,17},{2,18},{3,19},{4,20},{5,21},{6,22},{7,23},{8,24},{9,... | collective-permute-start | bytes 589832 | tf_op jit(solution)/shard_map/ppermute | solution.py:307
  70.6 9.6 %collective-permute-start.3 = (bf16[128,768]{1,0:T(8,128)(2,1)}, bf16[128,768]{1,0:T(8,128)(2,1)S(1)}, u32[]{:S(2)}, u32[]{:S(2)}) collective-permute-start(bf16[128,768]{1,0:T(8,128)(2,1)} %get-tuple-element.18), channel_id=1, source_target_pairs={{0,112},{1,113},{2,114},{3,115},{4,116},{5,117},{6,118},{7,119},{8... | collective-permute-start | bytes 589832 | tf_op jit(solution)/shard_map/ppermute | solution.py:316
  72.7 10.0 %collective-permute-start.19 = (f32[1,1536]{1,0:T(1,128)S(1)}, f32[1,1536]{1,0:T(1,128)S(1)}, u32[]{:S(2)}, u32[]{:S(2)}) collective-permute-start(f32[1,1536]{1,0:T(1,128)S(1)} %add_add_fusion), channel_id=1, source_target_pairs={{0,192},{1,193},{2,194},{3,195},{4,196},{5,197},{6,198},{7,199},{8... | collective-permute-start | bytes 18440 | tf_op jit(solution)/shard_map/ppermute | solution.py:327
  73.9 8.9 %collective-permute-start.18 = (f32[1,1536]{1,0:T(1,128)S(1)}, f32[1,1536]{1,0:T(1,128)S(1)}, u32[]{:S(2)}, u32[]{:S(2)}) collective-permute-start(f32[1,1536]{1,0:T(1,128)S(1)} %add_add_fusion), channel_id=1, source_target_pairs={{0,128},{1,129},{2,130},{3,131},{4,132},{5,133},{6,134},{7,135},{8... | collective-permute-start | bytes 18440 | tf_op jit(solution)/shard_map/ppermute | solution.py:327
  74.0 8.8 %collective-permute-start.17 = (f32[1,1536]{1,0:T(1,128)S(1)}, f32[1,1536]{1,0:T(1,128)S(1)}, u32[]{:S(2)}, u32[]{:S(2)}) collective-permute-start(f32[1,1536]{1,0:T(1,128)S(1)} %add_add_fusion), channel_id=1, source_target_pairs={{0,64},{1,65},{2,66},{3,67},{4,68},{5,69},{6,70},{7,71},{8,72},{9,... | collective-permute-start | bytes 18440 | tf_op jit(solution)/shard_map/ppermute | solution.py:327
  (6 other events, 9.0 us)

commit v2 on v1

v2 whole, which is shorter than its diff:
```python
import math

import jax
import jax.numpy as jnp
from jax import lax
from jax.experimental import pallas as pl
from jax.experimental.pallas import tpu as pltpu
from jax.sharding import PartitionSpec as P

TAPS = 5
EPS = 1e-06
ROWS = 128
CH = 1536
COUT = 768
PART = 768
PARTS = CH // PART
TILE = 256
ROOT = math.sqrt(2.0 / math.pi)
CUBE = 0.044715
FAR = (0, 4)
LANES = 128
PART_OUT = 512
BF = jnp.bfloat16
F32 = jnp.float32


def exchange_matrix():
    rows = lax.broadcasted_iota(jnp.int32, (TILE, TILE), 0)
    cols = lax.broadcasted_iota(jnp.int32, (TILE, TILE), 1)
    return jnp.where(rows + cols == TILE - 1, 1.0, 0.0).astype(BF)


def flip_tile(ref, tile, count, swap, rows=slice(None)):
    first = (count - 1 - tile) * TILE
    return jnp.dot(ref[rows, first : first + TILE], swap, preferred_element_type=F32)


def fetch(weight, taps, held, sems):
    copies = []
    for slot, tap in enumerate(taps):
        for part in range(PARTS):
            rows = pl.ds(part * PART, PART)
            copy = pltpu.make_async_copy(weight.at[tap, rows], held.at[slot, rows], sems.at[slot, part])
            copy.start()
            copies.append(copy)
    return copies


def partial_sums(stacked, held, sums, turned, slots):
    for place, slot in enumerate(slots):
        product = jnp.dot(stacked[...], held[slot], preferred_element_type=F32)
        sums[place] = product[:ROWS]
        turned[place] = product[ROWS:].astype(BF)


def outgoing(sums, turned, swap, spot, reach, to_a, to_b):
    even = lax.rem(spot, 2) == 0
    ahead_ok = spot + reach < 8
    behind_ok = spot - reach >= 0
    for tile in range(COUT // TILE):
        span = slice(tile * TILE, (tile + 1) * TILE)
        ahead = sums[0, :, span] + flip_tile(turned.at[1], tile, COUT // TILE, swap)
        behind = sums[1, :, span] + flip_tile(turned.at[0], tile, COUT // TILE, swap)
        ahead = jnp.where(ahead_ok, ahead, 0.0)
        behind = jnp.where(behind_ok, behind, 0.0)
        to_a[:, span] = jnp.where(even, ahead, behind).astype(to_a.dtype)
        to_b[:, span] = jnp.where(even, behind, ahead).astype(to_b.dtype)


def first_kernel(
    place, source, gain, weight, held, stacked, normed, slope, inv_rms, far_a, far_b, features, sums, turned, row_sem, sems
):
    load = pltpu.make_async_copy(source, features, row_sem)
    load.start()
    copies = fetch(weight, FAR, held, sems)
    swap = exchange_matrix()
    load.wait()
    wide = features[...].astype(F32)
    scale = lax.rsqrt(jnp.mean(wide * wide, axis=-1, keepdims=True) + EPS)
    inv_rms[...] = scale
    for lane in range(CH // LANES):
        span = slice(lane * LANES, (lane + 1) * LANES)
        value = features[:, span].astype(F32) * scale
        normed[:, span] = value
        scaled = value * gain[lane : lane + 1]
        square = scaled * scaled
        bend = jnp.tanh(ROOT * (scaled + CUBE * (square * scaled)))
        stacked[:ROWS, span] = (0.5 * scaled * (1.0 + bend)).astype(BF)
        slope[:, span] = 0.5 * (1.0 + bend) + 0.5 * scaled * (1.0 - bend * bend) * (
            ROOT * (1.0 + 3.0 * CUBE * square)
        )
    for tile in range(CH // TILE):
        span = slice(tile * TILE, (tile + 1) * TILE)
        stacked[ROWS:, span] = flip_tile(stacked, tile, CH // TILE, swap, slice(0, ROWS)).astype(BF)
    for copy in copies:
        copy.wait()
    partial_sums(stacked, held, sums, turned, (0, 1))
    outgoing(sums, turned, swap, place[0], 2, far_a, far_b)


def middle_kernel(place, stacked, weight, grad, grad_a, grad_b, near_a, near_b, own, total, sums, turned, lhs):
    swap = exchange_matrix()
    spot = place[0]
    even = lax.rem(spot, 2) == 0
    lhs[1, :ROWS] = grad[...]
    for tile in range(COUT // TILE):
        span = slice(tile * TILE, (tile + 1) * TILE)
        lhs[1, ROWS:, span] = flip_tile(grad, tile, COUT // TILE, swap).astype(BF)
    stack_pair(lhs, even, spot + 1 < 8, spot - 1 >= 0, grad_a, grad_b, 0, 2, swap)
    partial_sums(stacked, weight, sums, turned, (2,))
    for tile in range(COUT // TILE):
        span = slice(tile * TILE, (tile + 1) * TILE)
        own[:, span] = sums[0, :, span] + flip_tile(turned.at[0], tile, COUT // TILE, swap)
    partial_sums(stacked, weight, sums, turned, (1, 3))
    outgoing(sums, turned, swap, spot, 1, near_a, near_b)
    for part in range(CH // PART_OUT):
        span = slice(part * PART_OUT, (part + 1) * PART_OUT)
        total[:, span] = (
            pull_back(lhs[0], weight[1, span])
            + pull_back(lhs[1], weight[2, span])
            + pull_back(lhs[2], weight[3, span])
        )


def relay_kernel(near_a, near_b, from_a, from_b, to_a, to_b):
    to_a[...] = (near_a[...] + from_b[...].astype(F32)).astype(BF)
    to_b[...] = (near_b[...] + from_a[...].astype(F32)).astype(BF)


def join_kernel(own, from_a, from_b, convolved):
    convolved[...] = (own[...] + (from_a[...].astype(F32) + from_b[...].astype(F32))).astype(BF)


def stack_pair(lhs, even, ok_ahead, ok_behind, first, second, tap_low, tap_high, swap):
    zero = jnp.zeros((ROWS, COUT), BF)
    for flag, ahead_ref, behind_ref in ((True, first, second), (False, second, first)):

        @pl.when(even if flag else jnp.logical_not(even))
        def _(ahead_ref=ahead_ref, behind_ref=behind_ref):
            lhs[tap_low, :ROWS] = jnp.where(ok_ahead, ahead_ref[...], zero)
            lhs[tap_high, :ROWS] = jnp.where(ok_behind, behind_ref[...], zero)

    for tile in range(COUT // TILE):
        span = slice(tile * TILE, (tile + 1) * TILE)
        lhs[tap_low, ROWS:, span] = flip_tile(lhs.at[tap_high], tile, COUT // TILE, swap, slice(0, ROWS)).astype(BF)
        lhs[tap_high, ROWS:, span] = flip_tile(lhs.at[tap_low], tile, COUT // TILE, swap, slice(0, ROWS)).astype(BF)


def pull_back(rows, weight):
    return lax.dot_general(rows, weight, (((1,), (1,)), ((), ())), preferred_element_type=F32)


def last_kernel(place, from_a, from_b, held, near, normed, gain, slope, inv_rms, grad, gain_part, total, lhs, turned):
    swap = exchange_matrix()
    spot = place[0]
    even = lax.rem(spot, 2) == 0
    stack_pair(lhs, even, spot + 2 < 8, spot - 2 >= 0, from_a, from_b, 0, 1, swap)
    for part in range(CH // PART_OUT):
        span = slice(part * PART_OUT, (part + 1) * PART_OUT)
        term = near[:, span] + pull_back(lhs[0], held[0, span]) + pull_back(lhs[1], held[1, span])
        total[:, span] = term[:ROWS]
        turned[:, span] = term[ROWS:].astype(BF)
    spread = jnp.zeros((ROWS, 1), F32)
    for tile in range(CH // TILE):
        flipped = flip_tile(turned, tile, CH // TILE, swap)
        for half in range(TILE // LANES):
            lane = tile * (TILE // LANES) + half
            span = slice(lane * LANES, (lane + 1) * LANES)
            hidden_grad = total[:, span] + flipped[:, half * LANES : (half + 1) * LANES]
            scaled_grad = hidden_grad * slope[:, span]
            product = scaled_grad * normed[:, span]
            gain_part[lane : lane + 1] = jnp.sum(product, axis=0, keepdims=True)
            spread = spread + jnp.sum(product * gain[lane : lane + 1], axis=-1, keepdims=True)
            total[:, span] = scaled_grad * gain[lane : lane + 1]
    spread = spread * (1.0 / CH)
    scale = inv_rms[...]
    for tile in range(CH // TILE):
        span = slice(tile * TILE, (tile + 1) * TILE)
        grad[:, span] = (scale * (total[:, span] - normed[:, span] * spread)).astype(BF)


VMEM = pl.BlockSpec(memory_space=pltpu.VMEM)
SMEM = pl.BlockSpec(memory_space=pltpu.SMEM)
HBM = pl.BlockSpec(memory_space=pl.ANY)
LIMIT = pltpu.CompilerParams(vmem_limit_bytes=24 * 2**20)


def shape(dims, kind):
    return jax.ShapeDtypeStruct(dims, kind)


def remote(value):
    return pltpu.with_memory_space_constraint(value, pltpu.HBM)


def local(value):
    return pltpu.with_memory_space_constraint(value, pltpu.VMEM)


def first(place, features, gain, weight):
    return pl.pallas_call(
        first_kernel,
        out_shape=(
            pltpu.VMEM((2, CH, COUT), BF),
            pltpu.VMEM((2 * ROWS, CH), BF),
            pltpu.VMEM((ROWS, CH), F32),
            pltpu.VMEM((ROWS, CH), F32),
            pltpu.VMEM((ROWS, 1), F32),
            pltpu.VMEM((ROWS, COUT), BF),
            pltpu.VMEM((ROWS, COUT), BF),
        ),
        in_specs=[SMEM, HBM, VMEM, HBM],
        out_specs=[VMEM] * 7,
        scratch_shapes=[
            pltpu.VMEM((ROWS, CH), BF),
            pltpu.VMEM((2, ROWS, COUT), F32),
            pltpu.VMEM((2, ROWS, COUT), BF),
            pltpu.SemaphoreType.DMA,
            pltpu.SemaphoreType.DMA((2, PARTS)),
        ],
        compiler_params=LIMIT,
        cost_estimate=pl.CostEstimate(flops=1300000000, bytes_accessed=6000000, transcendentals=200000),
        name="first",
    )(place, remote(features), local(gain), remote(weight))


def middle(place, stacked, weight, grad, grad_a, grad_b):
    return pl.pallas_call(
        middle_kernel,
        out_shape=(
            pltpu.VMEM((ROWS, COUT), F32),
            pltpu.VMEM((ROWS, COUT), F32),
            pltpu.VMEM((ROWS, COUT), F32),
            pltpu.VMEM((2 * ROWS, CH), F32),
        ),
        in_specs=[SMEM] + [VMEM] * 5,
        out_specs=[VMEM] * 4,
        scratch_shapes=[
            pltpu.VMEM((2, ROWS, COUT), F32),
            pltpu.VMEM((2, ROWS, COUT), BF),
            pltpu.VMEM((3, 2 * ROWS, COUT), BF),
        ],
        compiler_params=LIMIT,
        cost_estimate=pl.CostEstimate(flops=3600000000, bytes_accessed=8000000, transcendentals=0),
        name="middle",
    )(place, local(stacked), local(weight), local(grad), local(grad_a), local(grad_b))


def last(place, from_a, from_b, held, near, normed, gain, slope, inv_rms):
    return pl.pallas_call(
        last_kernel,
        out_shape=(shape((ROWS, CH), BF), pltpu.VMEM((CH // LANES, LANES), F32)),
        in_specs=[SMEM] + [VMEM] * 8,
        out_specs=[VMEM] * 2,
        scratch_shapes=[
            pltpu.VMEM((ROWS, CH), F32),
            pltpu.VMEM((2, 2 * ROWS, COUT), BF),
            pltpu.VMEM((ROWS, CH), BF),
        ],
        compiler_params=LIMIT,
        cost_estimate=pl.CostEstimate(flops=1300000000, bytes_accessed=1000000, transcendentals=0),
        name="last",
    )(place, *(local(value) for value in (from_a, from_b, held, near, normed, gain, slope, inv_rms)))


def relay(near_a, near_b, from_a, from_b):
    return pl.pallas_call(
        relay_kernel,
        out_shape=(pltpu.VMEM((ROWS, COUT), BF), pltpu.VMEM((ROWS, COUT), BF)),
        in_specs=[VMEM] * 4,
        out_specs=[VMEM] * 2,
        compiler_params=LIMIT,
        cost_estimate=pl.CostEstimate(flops=400000, bytes_accessed=1000000, transcendentals=0),
        name="relay",
    )(local(near_a), local(near_b), local(from_a), local(from_b))


def join(own, from_a, from_b):
    return pl.pallas_call(
        join_kernel,
        out_shape=shape((ROWS, COUT), BF),
        in_specs=[VMEM] * 3,
        out_specs=VMEM,
        compiler_params=LIMIT,
        cost_estimate=pl.CostEstimate(flops=200000, bytes_accessed=1000000, transcendentals=0),
        name="join",
    )(local(own), local(from_a), local(from_b))


def exchange_a(value):
    return lax.ppermute(value, "ctx", [(i, ((i // 16) ^ 1) * 16 + i % 16) for i in range(128)])


def exchange_b(value):
    pairs = []
    for i in range(128):
        spot = i // 16
        other = (spot + 1) % 8 if spot % 2 else (spot - 1) % 8
        pairs.append((i, other * 16 + i % 16))
    return lax.ppermute(value, "ctx", pairs)


BOTH = ("dp", "ctx")
DIGITS = {"core": (1, 2), "z": (2, 8), "y": (16, 4), "xh": (64, 2), "xl": (128, 2)}


def turn(value, **steps):
    pairs = []
    for i in range(256):
        target = i
        for name, step in steps.items():
            base, radix = DIGITS[name]
            digit = (i // base) % radix
            target += ((digit + step) % radix - digit) * base
        pairs.append((i, target))
    return lax.ppermute(value, BOTH, pairs)


def sum_everywhere(value):
    value = value + turn(value, core=1)
    low = turn(value, z=1)
    high = turn(value, z=-1)
    pair = value + high
    three = pair + low
    value = three + turn(three, z=3) + turn(pair, z=-2)
    value = value + turn(value, xl=1) + turn(value, xh=1) + turn(value, xl=1, xh=1)
    return value + turn(value, y=1) + turn(value, y=2) + turn(value, y=-1)


def per_device(features, gain, conv_weight, cotangent):
    spot = (lax.axis_index("ctx") // 16).astype(jnp.int32)
    place = spot.reshape(1)
    rows = features.reshape(ROWS, CH)
    gains = gain.reshape(CH // LANES, LANES)
    own = cotangent.reshape(ROWS, COUT)
    grad_a = exchange_a(own)
    grad_b = exchange_b(own)
    held, stacked, normed, slope, inv_rms, far_a, far_b = first(place, rows, gains, conv_weight)
    grad_a, grad_b, held = lax.optimization_barrier((grad_a, grad_b, held))
    grad_ba = exchange_a(grad_b)
    grad_ab = exchange_b(grad_a)
    near_a, near_b, center, near = middle(place, stacked, conv_weight, own, grad_a, grad_b)
    input_grad, gain_part = last(place, grad_ba, grad_ab, held, near, normed, gains, slope, inv_rms)
    to_a, to_b = relay(near_a, near_b, exchange_a(far_a), exchange_b(far_b))
    convolved = join(center, exchange_a(to_a), exchange_b(to_b))
    gain_grad = sum_everywhere(gain_part).reshape(CH) / math.sqrt(2 * 16384)
    return (
        convolved.reshape(1, ROWS, COUT),
        input_grad.reshape(1, ROWS, CH),
        gain_grad,
    )


def solution(mesh):
    return jax.shard_map(
        per_device,
        mesh=mesh,
        in_specs=(P("dp", "ctx", None), P(), P(), P("dp", "ctx", None)),
        out_specs=(P("dp", "ctx", None), P("dp", "ctx", None), P()),
        check_vma=False,
    )
```

time: 83.6 us -> 59.9 us (0.72)
  the two profiles are of different devices: /device:TPU:64 before, /device:TPU:8 now
where the time goes in v2:
time: 59.9 us; the launch traced here: 59.8 us
  starting transfers between devices  38.9 us (65%)
  Pallas kernels  13.9 us (23%)
  waiting for transfers between devices  4.91 us (8%)
  between operations  0.71 us (1%)
  local copies, waits for them, and re-layouts  0.7 us (1%)
  other arithmetic  0.62 us (1%)
    ppermute x11, starting transfers between devices, turn(): return lax.ppermute(value, BOTH, pairs)  22.4 us
    ppermute x4, starting transfers between devices, exchange_a(): lax.ppermute(value, 'ctx', [(i, (i // 16 ^ 1) * 16 + i % 16) for i in ran...  12.6 us
    pallas_call x1, Pallas kernels, middle(): pl.pallas_call(middle_kernel, out_shape=(pltpu.VMEM((ROWS, COUT), F32), p...  5.29 us
    ppermute x11, waiting for transfers between devices, turn(): return lax.ppermute(value, BOTH, pairs)  4.89 us
    pallas_call x1, Pallas kernels, first(): pl.pallas_call(first_kernel, out_shape=(pltpu.VMEM((2, CH, COUT), BF), pl...  4.77 us
    ppermute x4, starting transfers between devices, exchange_b(): return lax.ppermute(value, 'ctx', pairs)  3.94 us
    pallas_call x1, Pallas kernels, last(): pl.pallas_call(last_kernel, out_shape=(shape((ROWS, CH), BF), pltpu.VMEM(...  2.97 us
  transfers between devices with their start and end apart: 19, of which 5 were waited for; matrix products, arithmetic and copies ran while one was open for 0% of the time, Pallas kernels for 18%

profile of v2, /device:TPU:8, one launch (start us, length us, event | category | flops | bytes accessed | tf_op | source)
XLA Modules:
  0.0 59.8 jit_solution(16480169351897662437)
XLA Ops:
  0.6 2.3 %collective-permute-start = (bf16[128,768]{1,0:T(8,128)(2,1)}, bf16[128,768]{1,0:T(8,128)(2,1)S(1)}, u32[]{:S(2)}, u32[]{:S(2)}) collective-permute-start(bf16[128,768]{1,0:T(8,128)(2,1)} %bitcast.10), channel_id=1, source_target_pairs={{0,16},{1,17},{2,18},{3,19},{4,20},{5,21},{6,22},{7,23},{8,24},{9,... | collective-permute-start | bytes 589832 | tf_op jit(solution)/shard_map/ppermute | solution.py:291
  2.9 0.7 %collective-permute-start.1 = (bf16[128,768]{1,0:T(8,128)(2,1)}, bf16[128,768]{1,0:T(8,128)(2,1)S(1)}, u32[]{:S(2)}, u32[]{:S(2)}) collective-permute-start(bf16[128,768]{1,0:T(8,128)(2,1)} %bitcast.11), channel_id=1, source_target_pairs={{0,112},{1,113},{2,114},{3,115},{4,116},{5,117},{6,118},{7,119},{8... | collective-permute-start | bytes 589832 | tf_op jit(solution)/shard_map/ppermute | solution.py:300
  3.6 0.7 %copy-done.1 = f32[1536]{0:T(1024)S(1)} copy-done((f32[1536]{0:T(1024)S(1)}, f32[1536]{0:T(1024)}, u32[]{:S(2)}) %copy-start.1) | copy-done | bytes 6168
  4.3 4.8 %first.1 = (bf16[2,1536,768]{2,1,0:T(8,128)(2,1)S(1)}, bf16[256,1536]{1,0:T(8,128)(2,1)S(1)}, f32[128,1536]{1,0:T(8,128)S(1)}, f32[128,1536]{1,0:T(8,128)S(1)}, ...) custom-call(s32[1]{0:T(128)} %bitcast.place, bf16[128,1536]{1,0:T(8,128)(2,1)} %bitcast.13, ...), custom_call_target="tpu_custom_call" | custom-call | flops 1300000000 | bytes 6000000 | tf_op jit(solution)/shard_map/first/pallas_call | solution.py:201
  9.1 3.9 %collective-permute-start.6 = (bf16[128,768]{1,0:T(8,128)(2,1)S(1)}, bf16[128,768]{1,0:T(8,128)(2,1)S(1)}, u32[]{:S(2)}, u32[]{:S(2)}) collective-permute-start(bf16[128,768]{1,0:T(8,128)(2,1)S(1)} %collective-permute-done.1.grad_b), channel_id=1, source_target_pairs={{0,16},{1,17},{2,18},{3,19},{4,20},{5,21},{6,22},{7,23},{8,24},{9,... | collective-permute-start | bytes 589832 | tf_op jit(solution)/shard_map/ppermute | solution.py:291
  13.0 1.5 %collective-permute-start.7 = (bf16[128,768]{1,0:T(8,128)(2,1)S(1)}, bf16[128,768]{1,0:T(8,128)(2,1)S(1)}, u32[]{:S(2)}, u32[]{:S(2)}) collective-permute-start(bf16[128,768]{1,0:T(8,128)(2,1)S(1)} %collective-permute-done.grad_a), channel_id=1, source_target_pairs={{0,112},{1,113},{2,114},{3,115},{4,116},{5,117},{6,118},{7,119},{8... | collective-permute-start | bytes 589832 | tf_op jit(solution)/shard_map/ppermute | solution.py:300
  14.5 5.3 %middle.1 = (f32[128,768]{1,0:T(8,128)S(1)}, f32[128,768]{1,0:T(8,128)S(1)}, f32[128,768]{1,0:T(8,128)S(1)}, f32[256,1536]{1,0:T(8,128)S(1)}) custom-call(s32[1]{0:T(128)} %bitcast.place, bf16[256,1536]{1,0:T(8,128)(2,1)S(1)} %get-tuple-element.21.stacked, bf16[5,1536,768]{2,1,0:T(8,128)(2,1)S(1)} %copy-done, bf16[128,768]{1,0:T(8,128)(2,1)S(1)} %bitcast.12, ...), custom_call_target="tpu_custom_call" | custom-call | flops 3600000000 | bytes 8000000 | tf_op jit(solution)/shard_map/middle/pallas_call | solution.py:228
  19.8 3.0 %last.1 = (bf16[128,1536]{1,0:T(8,128)(2,1)}, f32[12,128]{1,0:T(8,128)S(1)}) custom-call(s32[1]{0:T(128)} %bitcast.place, bf16[128,768]{1,0:T(8,128)(2,1)S(1)} %collective-permute-done.6.from_a, bf16[128,768]{1,0:T(8,128)(2,1)S(1)} %collective-permute-done.7.from_b, bf16[2,1536,768]{2,1,0:T(8,128)(2,1)S(1)} %get-tuple-element.32.held, ...), custom_call_target="tpu_custom_call" | custom-call | flops 1300000000 | bytes 1000000 | tf_op jit(solution)/shard_map/last/pallas_call | solution.py:250
  22.8 1.2 %collective-permute-done.8 = f32[12,128]{1,0:T(8,128)S(1)} collective-permute-done((f32[12,128]{1,0:T(8,128)S(1)}, f32[12,128]{1,0:T(8,128)S(1)}, u32[]{:S(2)}, u32[]{:S(2)}) %collective-permute-start.8) | collective-permute-done | bytes 6176 | tf_op jit(solution)/shard_map/ppermute | solution.py:316
  24.0 1.9 %collective-permute-start.10 = (f32[12,128]{1,0:T(8,128)S(1)}, f32[12,128]{1,0:T(8,128)S(1)}, u32[]{:S(2)}, u32[]{:S(2)}) collective-permute-start(f32[12,128]{1,0:T(8,128)S(1)} %add.34), channel_id=1, source_target_pairs={{0,2},{1,3},{2,4},{3,5},{4,6},{5,7},{6,8},{7,9},{8,10},{9,11},{10,... | collective-permute-start | bytes 18440 | tf_op jit(solution)/shard_map/ppermute | solution.py:316
  25.9 3.9 %collective-permute-start.9 = (f32[12,128]{1,0:T(8,128)S(1)}, f32[12,128]{1,0:T(8,128)S(1)}, u32[]{:S(2)}, u32[]{:S(2)}) collective-permute-start(f32[12,128]{1,0:T(8,128)S(1)} %add.34), channel_id=1, source_target_pairs={{0,14},{1,15},{2,0},{3,1},{4,2},{5,3},{6,4},{7,5},{8,6},{9,7},{10,... | collective-permute-start | bytes 18440 | tf_op jit(solution)/shard_map/ppermute | solution.py:316
  29.8 1.6 %collective-permute-done.10 = f32[12,128]{1,0:T(8,128)S(1)} collective-permute-done((f32[12,128]{1,0:T(8,128)S(1)}, f32[12,128]{1,0:T(8,128)S(1)}, u32[]{:S(2)}, u32[]{:S(2)}) %collective-permute-start.10) | collective-permute-done | bytes 6176 | tf_op jit(solution)/shard_map/ppermute | solution.py:316
  31.5 5.1 %collective-permute-start.11 = (f32[12,128]{1,0:T(8,128)S(1)}, f32[12,128]{1,0:T(8,128)S(1)}, u32[]{:S(2)}, u32[]{:S(2)}) collective-permute-start(f32[12,128]{1,0:T(8,128)S(1)} %get-tuple-element.39), channel_id=1, source_target_pairs={{0,6},{1,7},{2,8},{3,9},{4,10},{5,11},{6,12},{7,13},{8,14},{9,15},... | collective-permute-start | bytes 18440 | tf_op jit(solution)/shard_map/ppermute | solution.py:316
  36.6 3.1 %collective-permute-start.2 = (bf16[128,768]{1,0:T(8,128)(2,1)S(1)}, bf16[128,768]{1,0:T(8,128)(2,1)S(1)}, u32[]{:S(2)}, u32[]{:S(2)}) collective-permute-start(bf16[128,768]{1,0:T(8,128)(2,1)S(1)} %get-tuple-element.28), channel_id=1, source_target_pairs={{0,16},{1,17},{2,18},{3,19},{4,20},{5,21},{6,22},{7,23},{8,24},{9,... | collective-permute-start | bytes 589832 | tf_op jit(solution)/shard_map/ppermute | solution.py:291
  39.7 0.9 %collective-permute-start.3 = (bf16[128,768]{1,0:T(8,128)(2,1)S(1)}, bf16[128,768]{1,0:T(8,128)(2,1)S(1)}, u32[]{:S(2)}, u32[]{:S(2)}) collective-permute-start(bf16[128,768]{1,0:T(8,128)(2,1)S(1)} %get-tuple-element.29), channel_id=1, source_target_pairs={{0,112},{1,113},{2,114},{3,115},{4,116},{5,117},{6,118},{7,119},{8... | collective-permute-start | bytes 589832 | tf_op jit(solution)/shard_map/ppermute | solution.py:300
  41.2 1.5 %collective-permute-start.13 = (f32[12,128]{1,0:T(8,128)S(1)}, f32[12,128]{1,0:T(8,128)S(1)}, u32[]{:S(2)}, u32[]{:S(2)}) collective-permute-start(f32[12,128]{1,0:T(8,128)S(1)} %add_add_fusion.1), channel_id=1, source_target_pairs={{0,128},{1,129},{2,130},{3,131},{4,132},{5,133},{6,134},{7,135},{8... | collective-permute-start | bytes 18440 | tf_op jit(solution)/shard_map/ppermute | solution.py:316
  42.6 2.7 %collective-permute-start.14 = (f32[12,128]{1,0:T(8,128)S(1)}, f32[12,128]{1,0:T(8,128)S(1)}, u32[]{:S(2)}, u32[]{:S(2)}) collective-permute-start(f32[12,128]{1,0:T(8,128)S(1)} %add_add_fusion.1), channel_id=1, source_target_pairs={{0,64},{1,65},{2,66},{3,67},{4,68},{5,69},{6,70},{7,71},{8,72},{9,... | collective-permute-start | bytes 18440 | tf_op jit(solution)/shard_map/ppermute | solution.py:316
  45.9 3.4 %collective-permute-start.4 = (bf16[128,768]{1,0:T(8,128)(2,1)S(1)}, bf16[128,768]{1,0:T(8,128)(2,1)S(1)}, u32[]{:S(2)}, u32[]{:S(2)}) collective-permute-start(bf16[128,768]{1,0:T(8,128)(2,1)S(1)} %get-tuple-element.30), channel_id=1, source_target_pairs={{0,16},{1,17},{2,18},{3,19},{4,20},{5,21},{6,22},{7,23},{8,24},{9,... | collective-permute-start | bytes 589832 | tf_op jit(solution)/shard_map/ppermute | solution.py:291
  49.3 0.8 %collective-permute-start.5 = (bf16[128,768]{1,0:T(8,128)(2,1)S(1)}, bf16[128,768]{1,0:T(8,128)(2,1)S(1)}, u32[]{:S(2)}, u32[]{:S(2)}) collective-permute-start(bf16[128,768]{1,0:T(8,128)(2,1)S(1)} %get-tuple-element.31), channel_id=1, source_target_pairs={{0,112},{1,113},{2,114},{3,115},{4,116},{5,117},{6,118},{7,119},{8... | collective-permute-start | bytes 589832 | tf_op jit(solution)/shard_map/ppermute | solution.py:300
  50.3 1.2 %collective-permute-start.16 = (f32[12,128]{1,0:T(8,128)S(1)}, f32[12,128]{1,0:T(8,128)S(1)}, u32[]{:S(2)}, u32[]{:S(2)}) collective-permute-start(f32[12,128]{1,0:T(8,128)S(1)} %add_add_fusion), channel_id=1, source_target_pairs={{0,16},{1,17},{2,18},{3,19},{4,20},{5,21},{6,22},{7,23},{8,24},{9,... | collective-permute-start | bytes 18440 | tf_op jit(solution)/shard_map/ppermute | solution.py:316
  51.4 4.1 %collective-permute-start.17 = (f32[12,128]{1,0:T(8,128)S(1)}, f32[12,128]{1,0:T(8,128)S(1)}, u32[]{:S(2)}, u32[]{:S(2)}) collective-permute-start(f32[12,128]{1,0:T(8,128)S(1)} %add_add_fusion), channel_id=1, source_target_pairs={{0,32},{1,33},{2,34},{3,35},{4,36},{5,37},{6,38},{7,39},{8,40},{9,... | collective-permute-start | bytes 18440 | tf_op jit(solution)/shard_map/ppermute | solution.py:316
  55.5 1.5 %collective-permute-start.18 = (f32[12,128]{1,0:T(8,128)S(1)}, f32[12,128]{1,0:T(8,128)S(1)}, u32[]{:S(2)}, u32[]{:S(2)}) collective-permute-start(f32[12,128]{1,0:T(8,128)S(1)} %add_add_fusion), channel_id=1, source_target_pairs={{0,48},{1,49},{2,50},{3,51},{4,52},{5,53},{6,54},{7,55},{8,56},{9,... | collective-permute-start | bytes 18440 | tf_op jit(solution)/shard_map/ppermute | solution.py:316
  57.0 0.7 %join.1 = bf16[128,768]{1,0:T(8,128)(2,1)} custom-call(f32[128,768]{1,0:T(8,128)S(1)} %get-tuple-element.25.own, bf16[128,768]{1,0:T(8,128)(2,1)S(1)} %collective-permute-done.4.from_a, bf16[128,768]{1,0:T(8,128)(2,1)S(1)} %collective-permute-done.5.from_b), custom_call_target="tpu_custom_call" | custom-call | flops 200000 | bytes 1000000 | tf_op jit(solution)/shard_map/join/pallas_call | solution.py:279
  57.7 1.4 %collective-permute-done.18 = f32[12,128]{1,0:T(8,128)S(1)} collective-permute-done((f32[12,128]{1,0:T(8,128)S(1)}, f32[12,128]{1,0:T(8,128)S(1)}, u32[]{:S(2)}, u32[]{:S(2)}) %collective-permute-start.18) | collective-permute-done | bytes 6176 | tf_op jit(solution)/shard_map/ppermute | solution.py:316
  (30 shorter events, 1.9 us)
Async XLA Ops:
  0.6 8.4 %collective-permute-start = (bf16[128,768]{1,0:T(8,128)(2,1)}, bf16[128,768]{1,0:T(8,128)(2,1)S(1)}, u32[]{:S(2)}, u32[]{:S(2)}) collective-permute-start(bf16[128,768]{1,0:T(8,128)(2,1)} %bitcast.10), channel_id=1, source_target_pairs={{0,16},{1,17},{2,18},{3,19},{4,20},{5,21},{6,22},{7,23},{8,24},{9,... | collective-permute-start | bytes 589832 | tf_op jit(solution)/shard_map/ppermute | solution.py:291
  2.9 6.2 %collective-permute-start.1 = (bf16[128,768]{1,0:T(8,128)(2,1)}, bf16[128,768]{1,0:T(8,128)(2,1)S(1)}, u32[]{:S(2)}, u32[]{:S(2)}) collective-permute-start(bf16[128,768]{1,0:T(8,128)(2,1)} %bitcast.11), channel_id=1, source_target_pairs={{0,112},{1,113},{2,114},{3,115},{4,116},{5,117},{6,118},{7,119},{8... | collective-permute-start | bytes 589832 | tf_op jit(solution)/shard_map/ppermute | solution.py:300
  3.6 0.7 %copy-start.1 = (f32[1536]{0:T(1024)S(1)}, f32[1536]{0:T(1024)}, u32[]{:S(2)}) copy-start(f32[1536]{0:T(1024)} %param.5) | copy-start | bytes 18436
  4.3 10.2 %copy-start = (bf16[5,1536,768]{2,1,0:T(8,128)(2,1)S(1)}, bf16[5,1536,768]{2,1,0:T(8,128)(2,1)}, u32[]{:S(2)}) copy-start(bf16[5,1536,768]{2,1,0:T(8,128)(2,1)} %weight.3) | copy-start | bytes 35389444
  4.3 10.2 %copy-start.2 = (bf16[1,128,768]{2,1,0:T(8,128)(2,1)S(1)}, bf16[1,128,768]{2,1,0:T(8,128)(2,1)}, u32[]{:S(2)}) copy-start(bf16[1,128,768]{2,1,0:T(8,128)(2,1)} %param.7) | copy-start | bytes 589828
  9.1 10.7 %collective-permute-start.6 = (bf16[128,768]{1,0:T(8,128)(2,1)S(1)}, bf16[128,768]{1,0:T(8,128)(2,1)S(1)}, u32[]{:S(2)}, u32[]{:S(2)}) collective-permute-start(bf16[128,768]{1,0:T(8,128)(2,1)S(1)} %collective-permute-done.1.grad_b), channel_id=1, source_target_pairs={{0,16},{1,17},{2,18},{3,19},{4,20},{5,21},{6,22},{7,23},{8,24},{9,... | collective-permute-start | bytes 589832 | tf_op jit(solution)/shard_map/ppermute | solution.py:291
  13.0 6.8 %collective-permute-start.7 = (bf16[128,768]{1,0:T(8,128)(2,1)S(1)}, bf16[128,768]{1,0:T(8,128)(2,1)S(1)}, u32[]{:S(2)}, u32[]{:S(2)}) collective-permute-start(bf16[128,768]{1,0:T(8,128)(2,1)S(1)} %collective-permute-done.grad_a), channel_id=1, source_target_pairs={{0,112},{1,113},{2,114},{3,115},{4,116},{5,117},{6,118},{7,119},{8... | collective-permute-start | bytes 589832 | tf_op jit(solution)/shard_map/ppermute | solution.py:300
  22.8 1.2 %collective-permute-start.8 = (f32[12,128]{1,0:T(8,128)S(1)}, f32[12,128]{1,0:T(8,128)S(1)}, u32[]{:S(2)}, u32[]{:S(2)}) collective-permute-start(f32[12,128]{1,0:T(8,128)S(1)} %get-tuple-element.38), channel_id=1, source_target_pairs={{0,1},{1,0},{2,3},{3,2},{4,5},{5,4},{6,7},{7,6},{8,9},{9,8},{10,11... | collective-permute-start | bytes 18440 | tf_op jit(solution)/shard_map/ppermute | solution.py:316
  24.0 7.5 %collective-permute-start.10 = (f32[12,128]{1,0:T(8,128)S(1)}, f32[12,128]{1,0:T(8,128)S(1)}, u32[]{:S(2)}, u32[]{:S(2)}) collective-permute-start(f32[12,128]{1,0:T(8,128)S(1)} %add.34), channel_id=1, source_target_pairs={{0,2},{1,3},{2,4},{3,5},{4,6},{5,7},{6,8},{7,9},{8,10},{9,11},{10,... | collective-permute-start | bytes 18440 | tf_op jit(solution)/shard_map/ppermute | solution.py:316
  25.9 5.6 %collective-permute-start.9 = (f32[12,128]{1,0:T(8,128)S(1)}, f32[12,128]{1,0:T(8,128)S(1)}, u32[]{:S(2)}, u32[]{:S(2)}) collective-permute-start(f32[12,128]{1,0:T(8,128)S(1)} %add.34), channel_id=1, source_target_pairs={{0,14},{1,15},{2,0},{3,1},{4,2},{5,3},{6,4},{7,5},{8,6},{9,7},{10,... | collective-permute-start | bytes 18440 | tf_op jit(solution)/shard_map/ppermute | solution.py:316
  31.5 9.1 %collective-permute-start.11 = (f32[12,128]{1,0:T(8,128)S(1)}, f32[12,128]{1,0:T(8,128)S(1)}, u32[]{:S(2)}, u32[]{:S(2)}) collective-permute-start(f32[12,128]{1,0:T(8,128)S(1)} %get-tuple-element.39), channel_id=1, source_target_pairs={{0,6},{1,7},{2,8},{3,9},{4,10},{5,11},{6,12},{7,13},{8,14},{9,15},... | collective-permute-start | bytes 18440 | tf_op jit(solution)/shard_map/ppermute | solution.py:316
  36.6 4.5 %collective-permute-start.12 = (f32[12,128]{1,0:T(8,128)S(1)}, f32[12,128]{1,0:T(8,128)S(1)}, u32[]{:S(2)}, u32[]{:S(2)}) collective-permute-start(f32[12,128]{1,0:T(8,128)S(1)} %get-tuple-element.40), channel_id=1, source_target_pairs={{0,12},{1,13},{2,14},{3,15},{4,0},{5,1},{6,2},{7,3},{8,4},{9,5},{1... | collective-permute-start | bytes 18440 | tf_op jit(solution)/shard_map/ppermute | solution.py:316
  36.6 9.3 %collective-permute-start.2 = (bf16[128,768]{1,0:T(8,128)(2,1)S(1)}, bf16[128,768]{1,0:T(8,128)(2,1)S(1)}, u32[]{:S(2)}, u32[]{:S(2)}) collective-permute-start(bf16[128,768]{1,0:T(8,128)(2,1)S(1)} %get-tuple-element.28), channel_id=1, source_target_pairs={{0,16},{1,17},{2,18},{3,19},{4,20},{5,21},{6,22},{7,23},{8,24},{9,... | collective-permute-start | bytes 589832 | tf_op jit(solution)/shard_map/ppermute | solution.py:291
  39.7 6.2 %collective-permute-start.3 = (bf16[128,768]{1,0:T(8,128)(2,1)S(1)}, bf16[128,768]{1,0:T(8,128)(2,1)S(1)}, u32[]{:S(2)}, u32[]{:S(2)}) collective-permute-start(bf16[128,768]{1,0:T(8,128)(2,1)S(1)} %get-tuple-element.29), channel_id=1, source_target_pairs={{0,112},{1,113},{2,114},{3,115},{4,116},{5,117},{6,118},{7,119},{8... | collective-permute-start | bytes 589832 | tf_op jit(solution)/shard_map/ppermute | solution.py:300
  41.2 9.0 %collective-permute-start.13 = (f32[12,128]{1,0:T(8,128)S(1)}, f32[12,128]{1,0:T(8,128)S(1)}, u32[]{:S(2)}, u32[]{:S(2)}) collective-permute-start(f32[12,128]{1,0:T(8,128)S(1)} %add_add_fusion.1), channel_id=1, source_target_pairs={{0,128},{1,129},{2,130},{3,131},{4,132},{5,133},{6,134},{7,135},{8... | collective-permute-start | bytes 18440 | tf_op jit(solution)/shard_map/ppermute | solution.py:316
  42.6 7.5 %collective-permute-start.14 = (f32[12,128]{1,0:T(8,128)S(1)}, f32[12,128]{1,0:T(8,128)S(1)}, u32[]{:S(2)}, u32[]{:S(2)}) collective-permute-start(f32[12,128]{1,0:T(8,128)S(1)} %add_add_fusion.1), channel_id=1, source_target_pairs={{0,64},{1,65},{2,66},{3,67},{4,68},{5,69},{6,70},{7,71},{8,72},{9,... | collective-permute-start | bytes 18440 | tf_op jit(solution)/shard_map/ppermute | solution.py:316
  45.4 4.9 %collective-permute-start.15 = (f32[12,128]{1,0:T(8,128)S(1)}, f32[12,128]{1,0:T(8,128)S(1)}, u32[]{:S(2)}, u32[]{:S(2)}) collective-permute-start(f32[12,128]{1,0:T(8,128)S(1)} %add_add_fusion.1), channel_id=1, source_target_pairs={{0,192},{1,193},{2,194},{3,195},{4,196},{5,197},{6,198},{7,199},{8... | collective-permute-start | bytes 18440 | tf_op jit(solution)/shard_map/ppermute | solution.py:316
  45.9 11.0 %collective-permute-start.4 = (bf16[128,768]{1,0:T(8,128)(2,1)S(1)}, bf16[128,768]{1,0:T(8,128)(2,1)S(1)}, u32[]{:S(2)}, u32[]{:S(2)}) collective-permute-start(bf16[128,768]{1,0:T(8,128)(2,1)S(1)} %get-tuple-element.30), channel_id=1, source_target_pairs={{0,16},{1,17},{2,18},{3,19},{4,20},{5,21},{6,22},{7,23},{8,24},{9,... | collective-permute-start | bytes 589832 | tf_op jit(solution)/shard_map/ppermute | solution.py:291
  49.3 7.7 %collective-permute-start.5 = (bf16[128,768]{1,0:T(8,128)(2,1)S(1)}, bf16[128,768]{1,0:T(8,128)(2,1)S(1)}, u32[]{:S(2)}, u32[]{:S(2)}) collective-permute-start(bf16[128,768]{1,0:T(8,128)(2,1)S(1)} %get-tuple-element.31), channel_id=1, source_target_pairs={{0,112},{1,113},{2,114},{3,115},{4,116},{5,117},{6,118},{7,119},{8... | collective-permute-start | bytes 589832 | tf_op jit(solution)/shard_map/ppermute | solution.py:300
  50.3 7.5 %collective-permute-start.16 = (f32[12,128]{1,0:T(8,128)S(1)}, f32[12,128]{1,0:T(8,128)S(1)}, u32[]{:S(2)}, u32[]{:S(2)}) collective-permute-start(f32[12,128]{1,0:T(8,128)S(1)} %add_add_fusion), channel_id=1, source_target_pairs={{0,16},{1,17},{2,18},{3,19},{4,20},{5,21},{6,22},{7,23},{8,24},{9,... | collective-permute-start | bytes 18440 | tf_op jit(solution)/shard_map/ppermute | solution.py:316
  51.4 6.3 %collective-permute-start.17 = (f32[12,128]{1,0:T(8,128)S(1)}, f32[12,128]{1,0:T(8,128)S(1)}, u32[]{:S(2)}, u32[]{:S(2)}) collective-permute-start(f32[12,128]{1,0:T(8,128)S(1)} %add_add_fusion), channel_id=1, source_target_pairs={{0,32},{1,33},{2,34},{3,35},{4,36},{5,37},{6,38},{7,39},{8,40},{9,... | collective-permute-start | bytes 18440 | tf_op jit(solution)/shard_map/ppermute | solution.py:316
  55.5 3.7 %collective-permute-start.18 = (f32[12,128]{1,0:T(8,128)S(1)}, f32[12,128]{1,0:T(8,128)S(1)}, u32[]{:S(2)}, u32[]{:S(2)}) collective-permute-start(f32[12,128]{1,0:T(8,128)S(1)} %add_add_fusion), channel_id=1, source_target_pairs={{0,48},{1,49},{2,50},{3,51},{4,52},{5,53},{6,54},{7,55},{8,56},{9,... | collective-permute-start | bytes 18440 | tf_op jit(solution)/shard_map/ppermute | solution.py:316

commit v3 on v2

--- a/solution.py
+++ b/solution.py
@@ -19,6 +19,7 @@
 CUBE = 0.044715
 FAR = (0, 4)
 LANES = 128
+GROUP = 16
 PART_OUT = 512
 BF = jnp.bfloat16
 F32 = jnp.float32
@@ -68,16 +69,36 @@
 
 
 def first_kernel(
-    place, source, gain, weight, held, stacked, normed, slope, inv_rms, far_a, far_b, features, sums, turned, row_sem, sems
+    place,
+    source,
+    gain_source,
+    weight,
+    held,
+    stacked,
+    normed,
+    slope,
+    inv_rms,
+    far_a,
+    far_b,
+    gain,
+    features,
+    sums,
+    turned,
+    row_sem,
+    gain_sem,
+    sems,
 ):
     load = pltpu.make_async_copy(source, features, row_sem)
     load.start()
+    gain_load = pltpu.make_async_copy(gain_source, gain, gain_sem)
+    gain_load.start()
     copies = fetch(weight, FAR, held, sems)
     swap = exchange_matrix()
     load.wait()
     wide = features[...].astype(F32)
     scale = lax.rsqrt(jnp.mean(wide * wide, axis=-1, keepdims=True) + EPS)
     inv_rms[...] = scale
+    gain_load.wait()
     for lane in range(CH // LANES):
         span = slice(lane * LANES, (lane + 1) * LANES)
         value = features[:, span].astype(F32) * scale
@@ -98,7 +119,17 @@
     outgoing(sums, turned, swap, place[0], 2, far_a, far_b)
 
 
-def middle_kernel(place, stacked, weight, grad, grad_a, grad_b, near_a, near_b, own, total, sums, turned, lhs):
+def ahead_kernel(place, stacked, weight, near_a, near_b, own, sums, turned):
+    swap = exchange_matrix()
+    partial_sums(stacked, weight, sums, turned, (2,))
+    for tile in range(COUT // TILE):
+        span = slice(tile * TILE, (tile + 1) * TILE)
+        own[:, span] = sums[0, :, span] + flip_tile(turned.at[0], tile, COUT // TILE, swap)
+    partial_sums(stacked, weight, sums, turned, (1, 3))
+    outgoing(sums, turned, swap, place[0], 1, near_a, near_b)
+
+
+def back_kernel(place, grad, grad_b, grad_a, weight, total, lhs):
     swap = exchange_matrix()
     spot = place[0]
     even = lax.rem(spot, 2) == 0
@@ -107,12 +138,6 @@
         span = slice(tile * TILE, (tile + 1) * TILE)
         lhs[1, ROWS:, span] = flip_tile(grad, tile, COUT // TILE, swap).astype(BF)
     stack_pair(lhs, even, spot + 1 < 8, spot - 1 >= 0, grad_a, grad_b, 0, 2, swap)
-    partial_sums(stacked, weight, sums, turned, (2,))
-    for tile in range(COUT // TILE):
-        span = slice(tile * TILE, (tile + 1) * TILE)
-        own[:, span] = sums[0, :, span] + flip_tile(turned.at[0], tile, COUT // TILE, swap)
-    partial_sums(stacked, weight, sums, turned, (1, 3))
-    outgoing(sums, turned, swap, spot, 1, near_a, near_b)
     for part in range(CH // PART_OUT):
         span = slice(part * PART_OUT, (part + 1) * PART_OUT)
         total[:, span] = (
@@ -127,8 +152,9 @@
     to_b[...] = (near_b[...] + from_a[...].astype(F32)).astype(BF)
 
 
-def join_kernel(own, from_a, from_b, convolved):
+def join_kernel(own, from_a, from_b, terms, convolved, gain_grad):
     convolved[...] = (own[...] + (from_a[...].astype(F32) + from_b[...].astype(F32))).astype(BF)
+    gain_grad[...] = jnp.sum(terms[...], axis=0) * (1.0 / math.sqrt(2 * 16384))
 
 
 def stack_pair(lhs, even, ok_ahead, ok_behind, first, second, tap_low, tap_high, swap):
@@ -150,7 +176,7 @@
     return lax.dot_general(rows, weight, (((1,), (1,)), ((), ())), preferred_element_type=F32)
 
 
-def last_kernel(place, from_a, from_b, held, near, normed, gain, slope, inv_rms, grad, gain_part, total, lhs, turned):
+def last_kernel(place, from_b, from_a, held, near, normed, gain, slope, inv_rms, grad, gain_part, total, lhs, turned):
     swap = exchange_matrix()
     spot = place[0]
     even = lax.rem(spot, 2) == 0
@@ -169,7 +195,7 @@
             hidden_grad = total[:, span] + flipped[:, half * LANES : (half + 1) * LANES]
             scaled_grad = hidden_grad * slope[:, span]
             product = scaled_grad * normed[:, span]
-            gain_part[lane : lane + 1] = jnp.sum(product, axis=0, keepdims=True)
+            gain_part[:, lane : lane + 1] = jnp.broadcast_to(jnp.sum(product, axis=0, keepdims=True)[None], (GROUP, 1, LANES))
             spread = spread + jnp.sum(product * gain[lane : lane + 1], axis=-1, keepdims=True)
             total[:, span] = scaled_grad * gain[lane : lane + 1]
     spread = spread * (1.0 / CH)
@@ -208,48 +234,61 @@
             pltpu.VMEM((ROWS, 1), F32),
             pltpu.VMEM((ROWS, COUT), BF),
             pltpu.VMEM((ROWS, COUT), BF),
+            pltpu.VMEM((CH // LANES, LANES), F32),
         ),
-        in_specs=[SMEM, HBM, VMEM, HBM],
-        out_specs=[VMEM] * 7,
+        in_specs=[SMEM, HBM, HBM, HBM],
+        out_specs=[VMEM] * 8,
         scratch_shapes=[
             pltpu.VMEM((ROWS, CH), BF),
             pltpu.VMEM((2, ROWS, COUT), F32),
             pltpu.VMEM((2, ROWS, COUT), BF),
             pltpu.SemaphoreType.DMA,
+            pltpu.SemaphoreType.DMA,
             pltpu.SemaphoreType.DMA((2, PARTS)),
         ],
         compiler_params=LIMIT,
         cost_estimate=pl.CostEstimate(flops=1300000000, bytes_accessed=6000000, transcendentals=200000),
         name="first",
-    )(place, remote(features), local(gain), remote(weight))
-
-
-def middle(place, stacked, weight, grad, grad_a, grad_b):
-    return pl.pallas_call(
-        middle_kernel,
+    )(place, remote(features), remote(gain), remote(weight))
+
+
+def ahead(place, stacked, weight):
+    return pl.pallas_call(
+        ahead_kernel,
         out_shape=(
             pltpu.VMEM((ROWS, COUT), F32),
             pltpu.VMEM((ROWS, COUT), F32),
             pltpu.VMEM((ROWS, COUT), F32),
-            pltpu.VMEM((2 * ROWS, CH), F32),
         ),
-        in_specs=[SMEM] + [VMEM] * 5,
-        out_specs=[VMEM] * 4,
+        in_specs=[SMEM] + [VMEM] * 2,
+        out_specs=[VMEM] * 3,
         scratch_shapes=[
             pltpu.VMEM((2, ROWS, COUT), F32),
             pltpu.VMEM((2, ROWS, COUT), BF),
-            pltpu.VMEM((3, 2 * ROWS, COUT), BF),
         ],
         compiler_params=LIMIT,
-        cost_estimate=pl.CostEstimate(flops=3600000000, bytes_accessed=8000000, transcendentals=0),
-        name="middle",
-    )(place, local(stacked), local(weight), local(grad), local(grad_a), local(grad_b))
-
-
-def last(place, from_a, from_b, held, near, normed, gain, slope, inv_rms):
+        cost_estimate=pl.CostEstimate(flops=1800000000, bytes_accessed=1000000, transcendentals=0),
+        name="ahead",
+    )(place, local(stacked), local(weight))
+
+
+def back(place, grad, grad_b, grad_a, weight):
+    return pl.pallas_call(
+        back_kernel,
+        out_shape=pltpu.VMEM((2 * ROWS, CH), F32),
+        in_specs=[SMEM] + [VMEM] * 4,
+        out_specs=VMEM,
+        scratch_shapes=[pltpu.VMEM((3, 2 * ROWS, COUT), BF)],
+        compiler_params=LIMIT,
+        cost_estimate=pl.CostEstimate(flops=1800000000, bytes_accessed=1000000, transcendentals=0),
+        name="back",
+    )(place, *(local(value) for value in (grad, grad_b, grad_a, weight)))
+
+
+def last(place, from_b, from_a, held, near, normed, gain, slope, inv_rms):
     return pl.pallas_call(
         last_kernel,
-        out_shape=(shape((ROWS, CH), BF), pltpu.VMEM((CH // LANES, LANES), F32)),
+        out_shape=(shape((ROWS, CH), BF), pltpu.VMEM((GROUP, CH // LANES, LANES), F32)),
         in_specs=[SMEM] + [VMEM] * 8,
         out_specs=[VMEM] * 2,
         scratch_shapes=[
@@ -260,7 +299,7 @@
         compiler_params=LIMIT,
         cost_estimate=pl.CostEstimate(flops=1300000000, bytes_accessed=1000000, transcendentals=0),
         name="last",
-    )(place, *(local(value) for value in (from_a, from_b, held, near, normed, gain, slope, inv_rms)))
+    )(place, *(local(value) for value in (from_b, from_a, held, near, normed, gain, slope, inv_rms)))
 
 
 def relay(near_a, near_b, from_a, from_b):
@@ -275,16 +314,32 @@
     )(local(near_a), local(near_b), local(from_a), local(from_b))
 
 
-def join(own, from_a, from_b):
+def join(*values):
     return pl.pallas_call(
         join_kernel,
-        out_shape=shape((ROWS, COUT), BF),
-        in_specs=[VMEM] * 3,
-        out_specs=VMEM,
+        out_shape=(shape((ROWS, COUT), BF), shape((CH // LANES, LANES), F32)),
+        in_specs=[VMEM] * 4,
+        out_specs=[VMEM] * 2,
         compiler_params=LIMIT,
         cost_estimate=pl.CostEstimate(flops=200000, bytes_accessed=1000000, transcendentals=0),
         name="join",
-    )(local(own), local(from_a), local(from_b))
+    )(*(local(value) for value in values))
+
+
+def collect_kernel(terms, copies):
+    copies[...] = jnp.broadcast_to(jnp.sum(terms[...], axis=0, keepdims=True), copies.shape)
+
+
+def collect(terms):
+    return pl.pallas_call(
+        collect_kernel,
+        out_shape=pltpu.VMEM((GROUP, CH // LANES, LANES), F32),
+        in_specs=[VMEM],
+        out_specs=VMEM,
+        compiler_params=LIMIT,
+        cost_estimate=pl.CostEstimate(flops=30000, bytes_accessed=200000, transcendentals=0),
+        name="collect",
+    )(local(terms))
 
 
 def exchange_a(value):
@@ -295,36 +350,24 @@
     pairs = []
     for i in range(128):
         spot = i // 16
-        other = (spot + 1) % 8 if spot % 2 else (spot - 1) % 8
-        pairs.append((i, other * 16 + i % 16))
+        if spot in (0, 7):
+            pairs.append((i, i ^ 1))
+        else:
+            other = spot + 1 if spot % 2 else spot - 1
+            pairs.append((i, other * 16 + i % 16))
     return lax.ppermute(value, "ctx", pairs)
 
 
 BOTH = ("dp", "ctx")
-DIGITS = {"core": (1, 2), "z": (2, 8), "y": (16, 4), "xh": (64, 2), "xl": (128, 2)}
-
-
-def turn(value, **steps):
-    pairs = []
-    for i in range(256):
-        target = i
-        for name, step in steps.items():
-            base, radix = DIGITS[name]
-            digit = (i // base) % radix
-            target += ((digit + step) % radix - digit) * base
-        pairs.append((i, target))
-    return lax.ppermute(value, BOTH, pairs)
-
-
-def sum_everywhere(value):
-    value = value + turn(value, core=1)
-    low = turn(value, z=1)
-    high = turn(value, z=-1)
-    pair = value + high
-    three = pair + low
-    value = three + turn(three, z=3) + turn(pair, z=-2)
-    value = value + turn(value, xl=1) + turn(value, xh=1) + turn(value, xl=1, xh=1)
-    return value + turn(value, y=1) + turn(value, y=2) + turn(value, y=-1)
+
+
+def trade(copies, groups):
+    return lax.all_to_all(copies, BOTH, 0, 0, axis_index_groups=groups, tiled=True)
+
+
+def sum_everywhere(copies):
+    terms = trade(copies, [list(range(first, first + GROUP)) for first in range(0, 256, GROUP)])
+    return trade(collect(terms), [list(range(first, 256, GROUP)) for first in range(GROUP)])
 
 
 def per_device(features, gain, conv_weight, cotangent):
@@ -333,21 +376,23 @@
     rows = features.reshape(ROWS, CH)
     gains = gain.reshape(CH // LANES, LANES)
     own = cotangent.reshape(ROWS, COUT)
+    grad_b = exchange_b(own)
     grad_a = exchange_a(own)
-    grad_b = exchange_b(own)
-    held, stacked, normed, slope, inv_rms, far_a, far_b = first(place, rows, gains, conv_weight)
-    grad_a, grad_b, held = lax.optimization_barrier((grad_a, grad_b, held))
+    held, stacked, normed, slope, inv_rms, far_a, far_b, gain_rows = first(place, rows, gains, conv_weight)
+    grad_a, held, stacked = lax.optimization_barrier((grad_a, held, stacked))
+    grad_ab = exchange_b(grad_a)
+    near_a, near_b, center = ahead(place, stacked, conv_weight)
+    grad_b, center = lax.optimization_barrier((grad_b, center))
     grad_ba = exchange_a(grad_b)
-    grad_ab = exchange_b(grad_a)
-    near_a, near_b, center, near = middle(place, stacked, conv_weight, own, grad_a, grad_b)
-    input_grad, gain_part = last(place, grad_ba, grad_ab, held, near, normed, gains, slope, inv_rms)
+    near = back(place, own, grad_b, grad_a, conv_weight)
+    input_grad, gain_part = last(place, grad_ab, grad_ba, held, near, normed, gain_rows, slope, inv_rms)
     to_a, to_b = relay(near_a, near_b, exchange_a(far_a), exchange_b(far_b))
-    convolved = join(center, exchange_a(to_a), exchange_b(to_b))
-    gain_grad = sum_everywhere(gain_part).reshape(CH) / math.sqrt(2 * 16384)
+    terms = sum_everywhere(gain_part)
+    convolved, gain_grad = join(center, exchange_a(to_a), exchange_b(to_b), terms)
     return (
         convolved.reshape(1, ROWS, COUT),
         input_grad.reshape(1, ROWS, CH),
-        gain_grad,
+        gain_grad.reshape(CH),
     )
 
 

time: 59.9 us -> 59 us (0.985)
  the two profiles are of different devices: /device:TPU:8 before, /device:TPU:1 now
where the time goes in v3:
time: 59 us; the launch traced here: 58.7 us
  starting transfers between devices  29.3 us (50%)
  Pallas kernels  14.5 us (25%)
  waiting for transfers between devices  14 us (24%)
  between operations  0.74 us (1%)
    all_to_all x2, starting transfers between devices, trade(): lax.all_to_all(copies, BOTH, 0, 0, axis_index_groups=groups, tiled=True)  19.4 us
    all_to_all x2, waiting for transfers between devices, trade(): lax.all_to_all(copies, BOTH, 0, 0, axis_index_groups=groups, tiled=True)  13.9 us
    ppermute x4, starting transfers between devices, exchange_a(): lax.ppermute(value, 'ctx', [(i, (i // 16 ^ 1) * 16 + i % 16) for i in ran...  5.83 us
    pallas_call x1, Pallas kernels, first(): pl.pallas_call(first_kernel, out_shape=(pltpu.VMEM((2, CH, COUT), BF), pl...  4.83 us
    ppermute x4, starting transfers between devices, exchange_b(): return lax.ppermute(value, 'ctx', pairs)  4.13 us
    pallas_call x1, Pallas kernels, last(): pl.pallas_call(last_kernel, out_shape=(shape((ROWS, CH), BF), pltpu.VMEM(...  3.01 us
    pallas_call x1, Pallas kernels, ahead(): pl.pallas_call(ahead_kernel, out_shape=(pltpu.VMEM((ROWS, COUT), F32), pl...  2.74 us
    pallas_call x1, Pallas kernels, back(): pl.pallas_call(back_kernel, out_shape=pltpu.VMEM((2 * ROWS, CH), F32), in...  2.45 us
  transfers between devices with their start and end apart: 10, of which 2 were waited for; matrix products, arithmetic and copies ran while one was open for 0% of the time, Pallas kernels for 23%

profile of v3, /device:TPU:1, one launch (start us, length us, event | category | flops | bytes accessed | tf_op | source)
XLA Modules:
  0.0 58.7 jit_solution(14242090762724969057)
XLA Ops:
  0.6 2.2 %collective-permute-start.1 = (bf16[128,768]{1,0:T(8,128)(2,1)}, bf16[128,768]{1,0:T(8,128)(2,1)S(1)}, u32[]{:S(2)}, u32[]{:S(2)}) collective-permute-start(bf16[128,768]{1,0:T(8,128)(2,1)} %bitcast.7), channel_id=1, source_target_pairs={{0,16},{1,17},{2,18},{3,19},{4,20},{5,21},{6,22},{7,23},{8,24},{9,... | collective-permute-start | bytes 589832 | tf_op jit(solution)/shard_map/ppermute | solution.py:346
  2.8 1.2 %collective-permute-start = (bf16[128,768]{1,0:T(8,128)(2,1)}, bf16[128,768]{1,0:T(8,128)(2,1)S(1)}, u32[]{:S(2)}, u32[]{:S(2)}) collective-permute-start(bf16[128,768]{1,0:T(8,128)(2,1)} %bitcast.8), channel_id=1, source_target_pairs={{0,1},{1,0},{2,3},{3,2},{4,5},{5,4},{6,7},{7,6},{8,9},{9,8},{10,11... | collective-permute-start | bytes 589832 | tf_op jit(solution)/shard_map/ppermute | solution.py:358
  4.1 4.8 %first.1 = (bf16[2,1536,768]{2,1,0:T(8,128)(2,1)S(1)}, bf16[256,1536]{1,0:T(8,128)(2,1)S(1)}, f32[128,1536]{1,0:T(8,128)S(1)}, f32[128,1536]{1,0:T(8,128)S(1)}, ...) custom-call(s32[1]{0:T(128)} %bitcast.1.place, ...), custom_call_target="tpu_custom_call" | custom-call | flops 1300000000 | bytes 6000000 | tf_op jit(solution)/shard_map/first/pallas_call | solution.py:227
  8.9 0.0 copy-start.1
  8.9 0.9 %collective-permute-start.6 = (bf16[128,768]{1,0:T(8,128)(2,1)S(1)}, bf16[128,768]{1,0:T(8,128)(2,1)S(1)}, u32[]{:S(2)}, u32[]{:S(2)}) collective-permute-start(bf16[128,768]{1,0:T(8,128)(2,1)S(1)} %collective-permute-done.1.grad_a), channel_id=1, source_target_pairs={{0,1},{1,0},{2,3},{3,2},{4,5},{5,4},{6,7},{7,6},{8,9},{9,8},{10,11... | collective-permute-start | bytes 589832 | tf_op jit(solution)/shard_map/ppermute | solution.py:358
  9.8 0.1 copy-done
  10.0 2.7 %ahead.1 = (f32[128,768]{1,0:T(8,128)S(1)}, f32[128,768]{1,0:T(8,128)S(1)}, f32[128,768]{1,0:T(8,128)S(1)}) custom-call(s32[1]{0:T(128)} %bitcast.1.place, bf16[256,1536]{1,0:T(8,128)(2,1)S(1)} %get-tuple-element.27.stacked, bf16[5,1536,768]{2,1,0:T(8,128)(2,1)S(1)} %copy-done), custom_call_target="tpu_custom_call" | custom-call | flops 1800000000 | bytes 1000000 | tf_op jit(solution)/shard_map/ahead/pallas_call | solution.py:256
  12.7 0.0 collective-permute-done.grad_b
  12.7 1.2 %collective-permute-start.7 = (bf16[128,768]{1,0:T(8,128)(2,1)S(1)}, bf16[128,768]{1,0:T(8,128)(2,1)S(1)}, u32[]{:S(2)}, u32[]{:S(2)}) collective-permute-start(bf16[128,768]{1,0:T(8,128)(2,1)S(1)} %collective-permute-done.grad_b), channel_id=1, source_target_pairs={{0,16},{1,17},{2,18},{3,19},{4,20},{5,21},{6,22},{7,23},{8,24},{9,... | collective-permute-start | bytes 589832 | tf_op jit(solution)/shard_map/ppermute | solution.py:346
  13.9 0.4 collective-permute-start.2
  14.3 1.6 %collective-permute-start.3 = (bf16[128,768]{1,0:T(8,128)(2,1)S(1)}, bf16[128,768]{1,0:T(8,128)(2,1)S(1)}, u32[]{:S(2)}, u32[]{:S(2)}) collective-permute-start(bf16[128,768]{1,0:T(8,128)(2,1)S(1)} %get-tuple-element.33), channel_id=1, source_target_pairs={{0,1},{1,0},{2,3},{3,2},{4,5},{5,4},{6,7},{7,6},{8,9},{9,8},{10,11... | collective-permute-start | bytes 589832 | tf_op jit(solution)/shard_map/ppermute | solution.py:358
  15.9 2.5 %back.1.near = f32[256,1536]{1,0:T(8,128)S(1)} custom-call(s32[1]{0:T(128)} %bitcast.1.place, bf16[128,768]{1,0:T(8,128)(2,1)S(1)} %bitcast.9, bf16[128,768]{1,0:T(8,128)(2,1)S(1)} %collective-permute-done.grad_b, bf16[128,768]{1,0:T(8,128)(2,1)S(1)} %collective-permute-done.1.grad_a, bf16[5,1536,768]{2,1,0:T(8,128)(2,1)S(1)} %copy-done), custom_call_target="tpu_custom_call" | custom-call | flops 1800000000 | bytes 1000000 | tf_op jit(solution)/shard_map/back/pallas_call | solution.py:276
  18.4 0.0 collective-permute-done.6.from_b
  18.4 3.0 %last.1 = (bf16[128,1536]{1,0:T(8,128)(2,1)}, f32[16,12,128]{2,1,0:T(8,128)}) custom-call(s32[1]{0:T(128)} %bitcast.1.place, bf16[128,768]{1,0:T(8,128)(2,1)S(1)} %collective-permute-done.6.from_b, bf16[128,768]{1,0:T(8,128)(2,1)S(1)} %collective-permute-done.7.from_a, bf16[2,1536,768]{2,1,0:T(8,128)(2,1)S(1)} %get-tuple-element.38.held, ...), custom_call_target="tpu_custom_call" | custom-call | flops 1300000000 | bytes 1000000 | tf_op jit(solution)/shard_map/last/pallas_call | solution.py:289
  21.4 11.3 %all-to-all-start = ((f32[16,12,128]{2,1,0:T(8,128)}), f32[16,12,128]{2,1,0:T(8,128)S(1)}, u32[]{:S(2)}, u32[]{:S(2)}) async-start(f32[16,12,128]{2,1,0:T(8,128)} %get-tuple-element.43), calls=%async_computation | async-start | bytes 262144 | tf_op jit(solution)/shard_map/all_to_all | solution.py:365
  32.7 0.0 collective-permute-done.2.from_a
  32.7 0.1 relay.1
  32.8 2.1 %collective-permute-start.4 = (bf16[128,768]{1,0:T(8,128)(2,1)S(1)}, bf16[128,768]{1,0:T(8,128)(2,1)S(1)}, u32[]{:S(2)}, u32[]{:S(2)}) collective-permute-start(bf16[128,768]{1,0:T(8,128)(2,1)S(1)} %get-tuple-element.34), channel_id=1, source_target_pairs={{0,16},{1,17},{2,18},{3,19},{4,20},{5,21},{6,22},{7,23},{8,24},{9,... | collective-permute-start | bytes 589832 | tf_op jit(solution)/shard_map/ppermute | solution.py:346
  34.8 0.4 collective-permute-start.5
  35.2 6.6 %all-to-all-done.terms = f32[16,12,128]{2,1,0:T(8,128)S(1)} async-done(((f32[16,12,128]{2,1,0:T(8,128)}), f32[16,12,128]{2,1,0:T(8,128)S(1)}, u32[]{:S(2)}, u32[]{:S(2)}) %all-to-all-start) | async-done | bytes 98336 | tf_op jit(solution)/shard_map/all_to_all | solution.py:365
  41.8 0.7 %collect.1 = f32[16,12,128]{2,1,0:T(8,128)} custom-call(f32[16,12,128]{2,1,0:T(8,128)S(1)} %all-to-all-done.terms), custom_call_target="tpu_custom_call" | custom-call | flops 30000 | bytes 200000 | tf_op jit(solution)/shard_map/collect/pallas_call | solution.py:334
  42.5 8.1 %all-to-all-start.1 = ((f32[16,12,128]{2,1,0:T(8,128)}), f32[16,12,128]{2,1,0:T(8,128)S(1)}, u32[]{:S(2)}, u32[]{:S(2)}) async-start(f32[16,12,128]{2,1,0:T(8,128)} %collect.1), calls=%async_computation.1 | async-start | bytes 262144 | tf_op jit(solution)/shard_map/all_to_all | solution.py:365
  50.7 7.3 %all-to-all-done.1.terms = f32[16,12,128]{2,1,0:T(8,128)S(1)} async-done(((f32[16,12,128]{2,1,0:T(8,128)}), f32[16,12,128]{2,1,0:T(8,128)S(1)}, u32[]{:S(2)}, u32[]{:S(2)}) %all-to-all-start.1) | async-done | bytes 98336 | tf_op jit(solution)/shard_map/all_to_all | solution.py:365
  58.0 0.7 %join.1 = (bf16[128,768]{1,0:T(8,128)(2,1)}, f32[12,128]{1,0:T(8,128)}) custom-call(f32[128,768]{1,0:T(8,128)S(1)} %get-tuple-element.29.own, bf16[128,768]{1,0:T(8,128)(2,1)S(1)} %collective-permute-done.4.from_a, bf16[128,768]{1,0:T(8,128)(2,1)S(1)} %collective-permute-done.5.from_b, f32[16,12,128]{2,1,0:T(8,128)S(1)} %all-to-all-done.1.terms), custom_call_target="tpu_custom_call" | custom-call | flops 200000 | bytes 1000000 | tf_op jit(solution)/shard_map/join/pallas_call | solution.py:318
  (7 shorter events, 0.0 us)
Async XLA Ops:
  0.6 8.3 %collective-permute-start.1 = (bf16[128,768]{1,0:T(8,128)(2,1)}, bf16[128,768]{1,0:T(8,128)(2,1)S(1)}, u32[]{:S(2)}, u32[]{:S(2)}) collective-permute-start(bf16[128,768]{1,0:T(8,128)(2,1)} %bitcast.7), channel_id=1, source_target_pairs={{0,16},{1,17},{2,18},{3,19},{4,20},{5,21},{6,22},{7,23},{8,24},{9,... | collective-permute-start | bytes 589832 | tf_op jit(solution)/shard_map/ppermute | solution.py:346
  2.8 9.9 %collective-permute-start = (bf16[128,768]{1,0:T(8,128)(2,1)}, bf16[128,768]{1,0:T(8,128)(2,1)S(1)}, u32[]{:S(2)}, u32[]{:S(2)}) collective-permute-start(bf16[128,768]{1,0:T(8,128)(2,1)} %bitcast.8), channel_id=1, source_target_pairs={{0,1},{1,0},{2,3},{3,2},{4,5},{5,4},{6,7},{7,6},{8,9},{9,8},{10,11... | collective-permute-start | bytes 589832 | tf_op jit(solution)/shard_map/ppermute | solution.py:358
  4.1 5.9 %copy-start = (bf16[5,1536,768]{2,1,0:T(8,128)(2,1)S(1)}, bf16[5,1536,768]{2,1,0:T(8,128)(2,1)}, u32[]{:S(2)}) copy-start(bf16[5,1536,768]{2,1,0:T(8,128)(2,1)} %weight.5) | copy-start | bytes 35389444
  8.9 7.0 %copy-start.1 = (bf16[1,128,768]{2,1,0:T(8,128)(2,1)S(1)}, bf16[1,128,768]{2,1,0:T(8,128)(2,1)}, u32[]{:S(2)}) copy-start(bf16[1,128,768]{2,1,0:T(8,128)(2,1)} %param.7) | copy-start | bytes 589828
  8.9 9.5 %collective-permute-start.6 = (bf16[128,768]{1,0:T(8,128)(2,1)S(1)}, bf16[128,768]{1,0:T(8,128)(2,1)S(1)}, u32[]{:S(2)}, u32[]{:S(2)}) collective-permute-start(bf16[128,768]{1,0:T(8,128)(2,1)S(1)} %collective-permute-done.1.grad_a), channel_id=1, source_target_pairs={{0,1},{1,0},{2,3},{3,2},{4,5},{5,4},{6,7},{7,6},{8,9},{9,8},{10,11... | collective-permute-start | bytes 589832 | tf_op jit(solution)/shard_map/ppermute | solution.py:358
  12.7 5.7 %collective-permute-start.7 = (bf16[128,768]{1,0:T(8,128)(2,1)S(1)}, bf16[128,768]{1,0:T(8,128)(2,1)S(1)}, u32[]{:S(2)}, u32[]{:S(2)}) collective-permute-start(bf16[128,768]{1,0:T(8,128)(2,1)S(1)} %collective-permute-done.grad_b), channel_id=1, source_target_pairs={{0,16},{1,17},{2,18},{3,19},{4,20},{5,21},{6,22},{7,23},{8,24},{9,... | collective-permute-start | bytes 589832 | tf_op jit(solution)/shard_map/ppermute | solution.py:346
  13.9 18.8 %collective-permute-start.2 = (bf16[128,768]{1,0:T(8,128)(2,1)S(1)}, bf16[128,768]{1,0:T(8,128)(2,1)S(1)}, u32[]{:S(2)}, u32[]{:S(2)}) collective-permute-start(bf16[128,768]{1,0:T(8,128)(2,1)S(1)} %get-tuple-element.32), channel_id=1, source_target_pairs={{0,16},{1,17},{2,18},{3,19},{4,20},{5,21},{6,22},{7,23},{8,24},{9,... | collective-permute-start | bytes 589832 | tf_op jit(solution)/shard_map/ppermute | solution.py:346
  14.3 18.4 %collective-permute-start.3 = (bf16[128,768]{1,0:T(8,128)(2,1)S(1)}, bf16[128,768]{1,0:T(8,128)(2,1)S(1)}, u32[]{:S(2)}, u32[]{:S(2)}) collective-permute-start(bf16[128,768]{1,0:T(8,128)(2,1)S(1)} %get-tuple-element.33), channel_id=1, source_target_pairs={{0,1},{1,0},{2,3},{3,2},{4,5},{5,4},{6,7},{7,6},{8,9},{9,8},{10,11... | collective-permute-start | bytes 589832 | tf_op jit(solution)/shard_map/ppermute | solution.py:358
  21.4 20.4 %all-to-all-start = ((f32[16,12,128]{2,1,0:T(8,128)}), f32[16,12,128]{2,1,0:T(8,128)S(1)}, u32[]{:S(2)}, u32[]{:S(2)}) async-start(f32[16,12,128]{2,1,0:T(8,128)} %get-tuple-element.43), calls=%async_computation | async-start | bytes 262144 | tf_op jit(solution)/shard_map/all_to_all | solution.py:365
  32.8 17.9 %collective-permute-start.4 = (bf16[128,768]{1,0:T(8,128)(2,1)S(1)}, bf16[128,768]{1,0:T(8,128)(2,1)S(1)}, u32[]{:S(2)}, u32[]{:S(2)}) collective-permute-start(bf16[128,768]{1,0:T(8,128)(2,1)S(1)} %get-tuple-element.34), channel_id=1, source_target_pairs={{0,16},{1,17},{2,18},{3,19},{4,20},{5,21},{6,22},{7,23},{8,24},{9,... | collective-permute-start | bytes 589832 | tf_op jit(solution)/shard_map/ppermute | solution.py:346
  34.8 15.8 %collective-permute-start.5 = (bf16[128,768]{1,0:T(8,128)(2,1)S(1)}, bf16[128,768]{1,0:T(8,128)(2,1)S(1)}, u32[]{:S(2)}, u32[]{:S(2)}) collective-permute-start(bf16[128,768]{1,0:T(8,128)(2,1)S(1)} %get-tuple-element.35), channel_id=1, source_target_pairs={{0,1},{1,0},{2,3},{3,2},{4,5},{5,4},{6,7},{7,6},{8,9},{9,8},{10,11... | collective-permute-start | bytes 589832 | tf_op jit(solution)/shard_map/ppermute | solution.py:358
  42.5 15.4 %all-to-all-start.1 = ((f32[16,12,128]{2,1,0:T(8,128)}), f32[16,12,128]{2,1,0:T(8,128)S(1)}, u32[]{:S(2)}, u32[]{:S(2)}) async-start(f32[16,12,128]{2,1,0:T(8,128)} %collect.1), calls=%async_computation.1 | async-start | bytes 262144 | tf_op jit(solution)/shard_map/all_to_all | solution.py:365

commit v4 on v3

--- a/solution.py
+++ b/solution.py
@@ -12,12 +12,9 @@
 ROWS = 128
 CH = 1536
 COUT = 768
-PART = 768
-PARTS = CH // PART
 TILE = 256
 ROOT = math.sqrt(2.0 / math.pi)
 CUBE = 0.044715
-FAR = (0, 4)
 LANES = 128
 GROUP = 16
 PART_OUT = 512
@@ -34,17 +31,6 @@
 def flip_tile(ref, tile, count, swap, rows=slice(None)):
     first = (count - 1 - tile) * TILE
     return jnp.dot(ref[rows, first : first + TILE], swap, preferred_element_type=F32)
-
-
-def fetch(weight, taps, held, sems):
-    copies = []
-    for slot, tap in enumerate(taps):
-        for part in range(PARTS):
-            rows = pl.ds(part * PART, PART)
-            copy = pltpu.make_async_copy(weight.at[tap, rows], held.at[slot, rows], sems.at[slot, part])
-            copy.start()
-            copies.append(copy)
-    return copies
 
 
 def partial_sums(stacked, held, sums, turned, slots):
@@ -68,31 +54,11 @@
         to_b[:, span] = jnp.where(even, behind, ahead).astype(to_b.dtype)
 
 
-def first_kernel(
-    place,
-    source,
-    gain_source,
-    weight,
-    held,
-    stacked,
-    normed,
-    slope,
-    inv_rms,
-    far_a,
-    far_b,
-    gain,
-    features,
-    sums,
-    turned,
-    row_sem,
-    gain_sem,
-    sems,
-):
+def first_kernel(source, gain_source, stacked, normed, slope, inv_rms, gain, features, row_sem, gain_sem):
     load = pltpu.make_async_copy(source, features, row_sem)
     load.start()
     gain_load = pltpu.make_async_copy(gain_source, gain, gain_sem)
     gain_load.start()
-    copies = fetch(weight, FAR, held, sems)
     swap = exchange_matrix()
     load.wait()
     wide = features[...].astype(F32)
@@ -113,14 +79,12 @@
     for tile in range(CH // TILE):
         span = slice(tile * TILE, (tile + 1) * TILE)
         stacked[ROWS:, span] = flip_tile(stacked, tile, CH // TILE, swap, slice(0, ROWS)).astype(BF)
-    for copy in copies:
-        copy.wait()
-    partial_sums(stacked, held, sums, turned, (0, 1))
+
+
+def ahead_kernel(place, stacked, weight, far_a, far_b, near_a, near_b, own, sums, turned):
+    swap = exchange_matrix()
+    partial_sums(stacked, weight, sums, turned, (0, 4))
     outgoing(sums, turned, swap, place[0], 2, far_a, far_b)
-
-
-def ahead_kernel(place, stacked, weight, near_a, near_b, own, sums, turned):
-    swap = exchange_matrix()
     partial_sums(stacked, weight, sums, turned, (2,))
     for tile in range(COUT // TILE):
         span = slice(tile * TILE, (tile + 1) * TILE)
@@ -183,7 +147,7 @@
     stack_pair(lhs, even, spot + 2 < 8, spot - 2 >= 0, from_a, from_b, 0, 1, swap)
     for part in range(CH // PART_OUT):
         span = slice(part * PART_OUT, (part + 1) * PART_OUT)
-        term = near[:, span] + pull_back(lhs[0], held[0, span]) + pull_back(lhs[1], held[1, span])
+        term = near[:, span] + pull_back(lhs[0], held[0, span]) + pull_back(lhs[1], held[4, span])
         total[:, span] = term[:ROWS]
         turned[:, span] = term[ROWS:].astype(BF)
     spread = jnp.zeros((ROWS, 1), F32)
@@ -223,51 +187,43 @@
     return pltpu.with_memory_space_constraint(value, pltpu.VMEM)
 
 
-def first(place, features, gain, weight):
+def first(features, gain):
     return pl.pallas_call(
         first_kernel,
         out_shape=(
-            pltpu.VMEM((2, CH, COUT), BF),
             pltpu.VMEM((2 * ROWS, CH), BF),
             pltpu.VMEM((ROWS, CH), F32),
             pltpu.VMEM((ROWS, CH), F32),
             pltpu.VMEM((ROWS, 1), F32),
+            pltpu.VMEM((CH // LANES, LANES), F32),
+        ),
+        in_specs=[HBM] * 2,
+        out_specs=[VMEM] * 5,
+        scratch_shapes=[pltpu.VMEM((ROWS, CH), BF), pltpu.SemaphoreType.DMA, pltpu.SemaphoreType.DMA],
+        compiler_params=LIMIT,
+        cost_estimate=pl.CostEstimate(flops=5000000, bytes_accessed=6000000, transcendentals=200000),
+        name="first",
+    )(remote(features), remote(gain))
+
+
+def ahead(place, stacked, weight):
+    return pl.pallas_call(
+        ahead_kernel,
+        out_shape=(
             pltpu.VMEM((ROWS, COUT), BF),
             pltpu.VMEM((ROWS, COUT), BF),
-            pltpu.VMEM((CH // LANES, LANES), F32),
-        ),
-        in_specs=[SMEM, HBM, HBM, HBM],
-        out_specs=[VMEM] * 8,
-        scratch_shapes=[
-            pltpu.VMEM((ROWS, CH), BF),
-            pltpu.VMEM((2, ROWS, COUT), F32),
-            pltpu.VMEM((2, ROWS, COUT), BF),
-            pltpu.SemaphoreType.DMA,
-            pltpu.SemaphoreType.DMA,
-            pltpu.SemaphoreType.DMA((2, PARTS)),
-        ],
-        compiler_params=LIMIT,
-        cost_estimate=pl.CostEstimate(flops=1300000000, bytes_accessed=6000000, transcendentals=200000),
-        name="first",
-    )(place, remote(features), remote(gain), remote(weight))
-
-
-def ahead(place, stacked, weight):
-    return pl.pallas_call(
-        ahead_kernel,
-        out_shape=(
             pltpu.VMEM((ROWS, COUT), F32),
             pltpu.VMEM((ROWS, COUT), F32),
             pltpu.VMEM((ROWS, COUT), F32),
         ),
         in_specs=[SMEM] + [VMEM] * 2,
-        out_specs=[VMEM] * 3,
+        out_specs=[VMEM] * 5,
         scratch_shapes=[
             pltpu.VMEM((2, ROWS, COUT), F32),
             pltpu.VMEM((2, ROWS, COUT), BF),
         ],
         compiler_params=LIMIT,
-        cost_estimate=pl.CostEstimate(flops=1800000000, bytes_accessed=1000000, transcendentals=0),
+        cost_estimate=pl.CostEstimate(flops=3000000000, bytes_accessed=1000000, transcendentals=0),
         name="ahead",
     )(place, local(stacked), local(weight))
 
@@ -378,14 +334,14 @@
     own = cotangent.reshape(ROWS, COUT)
     grad_b = exchange_b(own)
     grad_a = exchange_a(own)
-    held, stacked, normed, slope, inv_rms, far_a, far_b, gain_rows = first(place, rows, gains, conv_weight)
-    grad_a, held, stacked = lax.optimization_barrier((grad_a, held, stacked))
+    stacked, normed, slope, inv_rms, gain_rows = first(rows, gains)
+    grad_a, stacked = lax.optimization_barrier((grad_a, stacked))
     grad_ab = exchange_b(grad_a)
-    near_a, near_b, center = ahead(place, stacked, conv_weight)
+    far_a, far_b, near_a, near_b, center = ahead(place, stacked, conv_weight)
     grad_b, center = lax.optimization_barrier((grad_b, center))
     grad_ba = exchange_a(grad_b)
     near = back(place, own, grad_b, grad_a, conv_weight)
-    input_grad, gain_part = last(place, grad_ab, grad_ba, held, near, normed, gain_rows, slope, inv_rms)
+    input_grad, gain_part = last(place, grad_ab, grad_ba, conv_weight, near, normed, gain_rows, slope, inv_rms)
     to_a, to_b = relay(near_a, near_b, exchange_a(far_a), exchange_b(far_b))
     terms = sum_everywhere(gain_part)
     convolved, gain_grad = join(center, exchange_a(to_a), exchange_b(to_b), terms)

time: 59 us -> 63 us (1.068)
  local copies, waits for them, and re-layouts: 0.13 us -> 4.36 us
  waiting for transfers between devices: 14 us -> 16.1 us
  Pallas kernels: 14.5 us -> 13 us
  starting transfers between devices: 29.3 us -> 28.5 us
    unnamed x4 -> x6, local copies, waits for them, and re-layouts: 0.13 us -> 4.36 us
    all_to_all x2, starting transfers between devices: 19.4 us -> 17.2 us  [trade(): lax.all_to_all(copies, BOTH, 0, 0, axis_index_groups=groups, tiled=True)]
    ppermute x4, starting transfers between devices: 4.13 us -> 5.9 us  [exchange_b(): return lax.ppermute(value, 'ctx', pairs)]
    ppermute x4, waiting for transfers between devices: 0.01 us -> 1.66 us  [exchange_a(): lax.ppermute(value, 'ctx', [(i, (i // 16 ^ 1) * 16 + i % 16) for i in ran...]
    pallas_call x2, Pallas kernels: 7.57 us -> 6.11 us  [the longest x1 4.14 us: ahead(): pl.pallas_call(ahead_kernel, out_shape=(pltpu.VMEM((ROWS, COUT), BF), plt...]
  transfers between devices with their start and end apart: 10 -> 10, of which waited for: 2 -> 4; matrix products, arithmetic and copies ran while one was open for 0% -> 0% of each run, Pallas kernels for 23% -> 20%
where the time goes in v4:
time: 63 us; the launch traced here: 62.7 us
  starting transfers between devices  28.5 us (45%)
  waiting for transfers between devices  16.1 us (26%)
  Pallas kernels  13 us (21%)
  local copies, waits for them, and re-layouts  4.36 us (7%)
  between operations  0.73 us (1%)
    all_to_all x2, starting transfers between devices, trade(): lax.all_to_all(copies, BOTH, 0, 0, axis_index_groups=groups, tiled=True)  17.2 us
    all_to_all x2, waiting for transfers between devices, trade(): lax.all_to_all(copies, BOTH, 0, 0, axis_index_groups=groups, tiled=True)  14.4 us
    ppermute x4, starting transfers between devices, exchange_b(): return lax.ppermute(value, 'ctx', pairs)  5.9 us
    ppermute x4, starting transfers between devices, exchange_a(): lax.ppermute(value, 'ctx', [(i, (i // 16 ^ 1) * 16 + i % 16) for i in ran...  5.38 us
    unnamed x6, local copies, waits for them, and re-layouts  4.36 us
    pallas_call x1, Pallas kernels, ahead(): pl.pallas_call(ahead_kernel, out_shape=(pltpu.VMEM((ROWS, COUT), BF), plt...  4.14 us
    pallas_call x1, Pallas kernels, last(): pl.pallas_call(last_kernel, out_shape=(shape((ROWS, CH), BF), pltpu.VMEM(...  3 us
    pallas_call x1, Pallas kernels, back(): pl.pallas_call(back_kernel, out_shape=pltpu.VMEM((2 * ROWS, CH), F32), in...  2.45 us
  transfers between devices with their start and end apart: 10, of which 4 were waited for; matrix products, arithmetic and copies ran while one was open for 0% of the time, Pallas kernels for 20%

profile of v4, /device:TPU:1, one launch (start us, length us, event | category | flops | bytes accessed | tf_op | source)
XLA Modules:
  0.0 62.7 jit_solution(6039414409527067741)
XLA Ops:
  0.6 2.2 %collective-permute-start.1 = (bf16[128,768]{1,0:T(8,128)(2,1)}, bf16[128,768]{1,0:T(8,128)(2,1)S(1)}, u32[]{:S(2)}, u32[]{:S(2)}) collective-permute-start(bf16[128,768]{1,0:T(8,128)(2,1)} %bitcast.7), channel_id=1, source_target_pairs={{0,16},{1,17},{2,18},{3,19},{4,20},{5,21},{6,22},{7,23},{8,24},{9,... | collective-permute-start | bytes 589832 | tf_op jit(solution)/shard_map/ppermute | solution.py:302
  2.9 1.2 %collective-permute-start = (bf16[128,768]{1,0:T(8,128)(2,1)}, bf16[128,768]{1,0:T(8,128)(2,1)S(1)}, u32[]{:S(2)}, u32[]{:S(2)}) collective-permute-start(bf16[128,768]{1,0:T(8,128)(2,1)} %bitcast.8), channel_id=1, source_target_pairs={{0,1},{1,0},{2,3},{3,2},{4,5},{5,4},{6,7},{7,6},{8,9},{9,8},{10,11... | collective-permute-start | bytes 589832 | tf_op jit(solution)/shard_map/ppermute | solution.py:314
  4.1 2.0 %first.1 = (bf16[256,1536]{1,0:T(8,128)(2,1)S(1)}, f32[128,1536]{1,0:T(8,128)S(1)}, f32[128,1536]{1,0:T(8,128)S(1)}, f32[128,1]{1,0:T(8,128)S(1)}, f32[12,128]{1,0:T(8,128)S(1)}) custom-call(bf16[128,1536]{1,0:T(8,128)(2,1)} %bitcast.10, f32[12,128]{1,0:T(8,128)} %bitcast.11), custom_call_target="tpu_custom_call" | custom-call | flops 5000000 | bytes 6000000 | tf_op jit(solution)/shard_map/first/pallas_call | solution.py:191
  6.0 0.5 collective-permute-done.1.grad_a
  6.6 3.3 %collective-permute-start.6 = (bf16[128,768]{1,0:T(8,128)(2,1)S(1)}, bf16[128,768]{1,0:T(8,128)(2,1)S(1)}, u32[]{:S(2)}, u32[]{:S(2)}) collective-permute-start(bf16[128,768]{1,0:T(8,128)(2,1)S(1)} %collective-permute-done.1.grad_a), channel_id=1, source_target_pairs={{0,1},{1,0},{2,3},{3,2},{4,5},{5,4},{6,7},{7,6},{8,9},{9,8},{10,11... | collective-permute-start | bytes 589832 | tf_op jit(solution)/shard_map/ppermute | solution.py:314
  9.9 4.3 %copy-done = bf16[5,1536,768]{2,1,0:T(8,128)(2,1)S(1)} copy-done((bf16[5,1536,768]{2,1,0:T(8,128)(2,1)S(1)}, bf16[5,1536,768]{2,1,0:T(8,128)(2,1)}, u32[]{:S(2)}) %copy-start) | copy-done | bytes 11796504
  14.2 4.1 %ahead.1 = (bf16[128,768]{1,0:T(8,128)(2,1)S(1)}, bf16[128,768]{1,0:T(8,128)(2,1)S(1)}, f32[128,768]{1,0:T(8,128)S(1)}, f32[128,768]{1,0:T(8,128)S(1)}, f32[128,768]{1,0:T(8,128)S(1)}) custom-call(s32[1]{0:T(128)} %bitcast.1.place, bf16[256,1536]{1,0:T(8,128)(2,1)S(1)} %get-tuple-element.24.stacked, bf16[5,1536,768]{2,1,0:T(8,128)(2,1)S(1)} %copy-done), custom_call_target="tpu_custom_call" | custom-call | flops 3000000000 | bytes 1000000 | tf_op jit(solution)/shard_map/ahead/pallas_call | solution.py:210
  18.4 0.0 collective-permute-done.grad_b
  18.4 0.4 collective-permute-start.7
  18.7 1.2 %collective-permute-start.2 = (bf16[128,768]{1,0:T(8,128)(2,1)S(1)}, bf16[128,768]{1,0:T(8,128)(2,1)S(1)}, u32[]{:S(2)}, u32[]{:S(2)}) collective-permute-start(bf16[128,768]{1,0:T(8,128)(2,1)S(1)} %get-tuple-element.29), channel_id=1, source_target_pairs={{0,16},{1,17},{2,18},{3,19},{4,20},{5,21},{6,22},{7,23},{8,24},{9,... | collective-permute-start | bytes 589832 | tf_op jit(solution)/shard_map/ppermute | solution.py:302
  19.9 1.0 %collective-permute-start.3 = (bf16[128,768]{1,0:T(8,128)(2,1)S(1)}, bf16[128,768]{1,0:T(8,128)(2,1)S(1)}, u32[]{:S(2)}, u32[]{:S(2)}) collective-permute-start(bf16[128,768]{1,0:T(8,128)(2,1)S(1)} %get-tuple-element.30), channel_id=1, source_target_pairs={{0,1},{1,0},{2,3},{3,2},{4,5},{5,4},{6,7},{7,6},{8,9},{9,8},{10,11... | collective-permute-start | bytes 589832 | tf_op jit(solution)/shard_map/ppermute | solution.py:314
  21.0 2.5 %back.1.near = f32[256,1536]{1,0:T(8,128)S(1)} custom-call(s32[1]{0:T(128)} %bitcast.1.place, bf16[128,768]{1,0:T(8,128)(2,1)S(1)} %bitcast.9, bf16[128,768]{1,0:T(8,128)(2,1)S(1)} %collective-permute-done.grad_b, bf16[128,768]{1,0:T(8,128)(2,1)S(1)} %collective-permute-done.1.grad_a, bf16[5,1536,768]{2,1,0:T(8,128)(2,1)S(1)} %copy-done.1), custom_call_target="tpu_custom_call" | custom-call | flops 1800000000 | bytes 1000000 | tf_op jit(solution)/shard_map/back/pallas_call | solution.py:232
  23.4 1.1 %collective-permute-done.7.from_a = bf16[128,768]{1,0:T(8,128)(2,1)S(1)} collective-permute-done((bf16[128,768]{1,0:T(8,128)(2,1)S(1)}, bf16[128,768]{1,0:T(8,128)(2,1)S(1)}, u32[]{:S(2)}, u32[]{:S(2)}) %collective-permute-start.7) | collective-permute-done | bytes 196640 | tf_op jit(solution)/shard_map/ppermute | solution.py:302
  24.6 3.0 %last.1 = (bf16[128,1536]{1,0:T(8,128)(2,1)}, f32[16,12,128]{2,1,0:T(8,128)}) custom-call(s32[1]{0:T(128)} %bitcast.1.place, bf16[128,768]{1,0:T(8,128)(2,1)S(1)} %collective-permute-done.6.from_b, bf16[128,768]{1,0:T(8,128)(2,1)S(1)} %collective-permute-done.7.from_a, bf16[5,1536,768]{2,1,0:T(8,128)(2,1)S(1)} %copy-done.1, f32[256,1536]{1,0:T(8,128)S(1)} %back.1.near, ...), custom_call_target="tpu_custom_call" | custom-call | flops 1300000000 | bytes 1000000 | tf_op jit(solution)/shard_map/last/pallas_call | solution.py:245
  27.6 10.6 %all-to-all-start = ((f32[16,12,128]{2,1,0:T(8,128)}), f32[16,12,128]{2,1,0:T(8,128)S(1)}, u32[]{:S(2)}, u32[]{:S(2)}) async-start(f32[16,12,128]{2,1,0:T(8,128)} %get-tuple-element.39), calls=%async_computation | async-start | bytes 262144 | tf_op jit(solution)/shard_map/all_to_all | solution.py:321
  38.1 0.0 collective-permute-done.2.from_a
  38.2 0.1 relay.1
  38.2 1.6 %collective-permute-start.4 = (bf16[128,768]{1,0:T(8,128)(2,1)S(1)}, bf16[128,768]{1,0:T(8,128)(2,1)S(1)}, u32[]{:S(2)}, u32[]{:S(2)}) collective-permute-start(bf16[128,768]{1,0:T(8,128)(2,1)S(1)} %get-tuple-element.31), channel_id=1, source_target_pairs={{0,16},{1,17},{2,18},{3,19},{4,20},{5,21},{6,22},{7,23},{8,24},{9,... | collective-permute-start | bytes 589832 | tf_op jit(solution)/shard_map/ppermute | solution.py:302
  39.8 0.4 collective-permute-start.5
  40.2 7.1 %all-to-all-done.terms = f32[16,12,128]{2,1,0:T(8,128)S(1)} async-done(((f32[16,12,128]{2,1,0:T(8,128)}), f32[16,12,128]{2,1,0:T(8,128)S(1)}, u32[]{:S(2)}, u32[]{:S(2)}) %all-to-all-start) | async-done | bytes 98336 | tf_op jit(solution)/shard_map/all_to_all | solution.py:321
  47.3 0.7 %collect.1 = f32[16,12,128]{2,1,0:T(8,128)} custom-call(f32[16,12,128]{2,1,0:T(8,128)S(1)} %all-to-all-done.terms), custom_call_target="tpu_custom_call" | custom-call | flops 30000 | bytes 200000 | tf_op jit(solution)/shard_map/collect/pallas_call | solution.py:290
  48.0 6.6 %all-to-all-start.1 = ((f32[16,12,128]{2,1,0:T(8,128)}), f32[16,12,128]{2,1,0:T(8,128)S(1)}, u32[]{:S(2)}, u32[]{:S(2)}) async-start(f32[16,12,128]{2,1,0:T(8,128)} %collect.1), calls=%async_computation.1 | async-start | bytes 262144 | tf_op jit(solution)/shard_map/all_to_all | solution.py:321
  54.7 7.3 %all-to-all-done.1.terms = f32[16,12,128]{2,1,0:T(8,128)S(1)} async-done(((f32[16,12,128]{2,1,0:T(8,128)}), f32[16,12,128]{2,1,0:T(8,128)S(1)}, u32[]{:S(2)}, u32[]{:S(2)}) %all-to-all-start.1) | async-done | bytes 98336 | tf_op jit(solution)/shard_map/all_to_all | solution.py:321
  62.0 0.7 %join.1 = (bf16[128,768]{1,0:T(8,128)(2,1)}, f32[12,128]{1,0:T(8,128)}) custom-call(f32[128,768]{1,0:T(8,128)S(1)} %get-tuple-element.26.own, bf16[128,768]{1,0:T(8,128)(2,1)S(1)} %collective-permute-done.4.from_a, bf16[128,768]{1,0:T(8,128)(2,1)S(1)} %collective-permute-done.5.from_b, f32[16,12,128]{2,1,0:T(8,128)S(1)} %all-to-all-done.1.terms), custom_call_target="tpu_custom_call" | custom-call | flops 200000 | bytes 1000000 | tf_op jit(solution)/shard_map/join/pallas_call | solution.py:274
  (9 shorter events, 0.0 us)
Async XLA Ops:
  0.6 20.3 %copy-start.2 = (bf16[1,128,768]{2,1,0:T(8,128)(2,1)S(1)}, bf16[1,128,768]{2,1,0:T(8,128)(2,1)}, u32[]{:S(2)}) copy-start(bf16[1,128,768]{2,1,0:T(8,128)(2,1)} %param.7) | copy-start | bytes 589828
  0.6 5.9 %collective-permute-start.1 = (bf16[128,768]{1,0:T(8,128)(2,1)}, bf16[128,768]{1,0:T(8,128)(2,1)S(1)}, u32[]{:S(2)}, u32[]{:S(2)}) collective-permute-start(bf16[128,768]{1,0:T(8,128)(2,1)} %bitcast.7), channel_id=1, source_target_pairs={{0,16},{1,17},{2,18},{3,19},{4,20},{5,21},{6,22},{7,23},{8,24},{9,... | collective-permute-start | bytes 589832 | tf_op jit(solution)/shard_map/ppermute | solution.py:302
  2.9 15.5 %collective-permute-start = (bf16[128,768]{1,0:T(8,128)(2,1)}, bf16[128,768]{1,0:T(8,128)(2,1)S(1)}, u32[]{:S(2)}, u32[]{:S(2)}) collective-permute-start(bf16[128,768]{1,0:T(8,128)(2,1)} %bitcast.8), channel_id=1, source_target_pairs={{0,1},{1,0},{2,3},{3,2},{4,5},{5,4},{6,7},{7,6},{8,9},{9,8},{10,11... | collective-permute-start | bytes 589832 | tf_op jit(solution)/shard_map/ppermute | solution.py:314
  6.6 16.9 %collective-permute-start.6 = (bf16[128,768]{1,0:T(8,128)(2,1)S(1)}, bf16[128,768]{1,0:T(8,128)(2,1)S(1)}, u32[]{:S(2)}, u32[]{:S(2)}) collective-permute-start(bf16[128,768]{1,0:T(8,128)(2,1)S(1)} %collective-permute-done.1.grad_a), channel_id=1, source_target_pairs={{0,1},{1,0},{2,3},{3,2},{4,5},{5,4},{6,7},{7,6},{8,9},{9,8},{10,11... | collective-permute-start | bytes 589832 | tf_op jit(solution)/shard_map/ppermute | solution.py:314
  9.8 4.4 %copy-start = (bf16[5,1536,768]{2,1,0:T(8,128)(2,1)S(1)}, bf16[5,1536,768]{2,1,0:T(8,128)(2,1)}, u32[]{:S(2)}) copy-start(bf16[5,1536,768]{2,1,0:T(8,128)(2,1)} %held.1) | copy-start | bytes 35389444
  14.2 6.8 %copy-start.1 = (bf16[5,1536,768]{2,1,0:T(8,128)(2,1)S(1)}, bf16[5,1536,768]{2,1,0:T(8,128)(2,1)}, u32[]{:S(2)}) copy-start(bf16[5,1536,768]{2,1,0:T(8,128)(2,1)} %held.1) | copy-start | bytes 35389444
  18.4 6.2 %collective-permute-start.7 = (bf16[128,768]{1,0:T(8,128)(2,1)S(1)}, bf16[128,768]{1,0:T(8,128)(2,1)S(1)}, u32[]{:S(2)}, u32[]{:S(2)}) collective-permute-start(bf16[128,768]{1,0:T(8,128)(2,1)S(1)} %collective-permute-done.grad_b), channel_id=1, source_target_pairs={{0,16},{1,17},{2,18},{3,19},{4,20},{5,21},{6,22},{7,23},{8,24},{9,... | collective-permute-start | bytes 589832 | tf_op jit(solution)/shard_map/ppermute | solution.py:302
  18.7 19.4 %collective-permute-start.2 = (bf16[128,768]{1,0:T(8,128)(2,1)S(1)}, bf16[128,768]{1,0:T(8,128)(2,1)S(1)}, u32[]{:S(2)}, u32[]{:S(2)}) collective-permute-start(bf16[128,768]{1,0:T(8,128)(2,1)S(1)} %get-tuple-element.29), channel_id=1, source_target_pairs={{0,16},{1,17},{2,18},{3,19},{4,20},{5,21},{6,22},{7,23},{8,24},{9,... | collective-permute-start | bytes 589832 | tf_op jit(solution)/shard_map/ppermute | solution.py:302
  19.9 18.2 %collective-permute-start.3 = (bf16[128,768]{1,0:T(8,128)(2,1)S(1)}, bf16[128,768]{1,0:T(8,128)(2,1)S(1)}, u32[]{:S(2)}, u32[]{:S(2)}) collective-permute-start(bf16[128,768]{1,0:T(8,128)(2,1)S(1)} %get-tuple-element.30), channel_id=1, source_target_pairs={{0,1},{1,0},{2,3},{3,2},{4,5},{5,4},{6,7},{7,6},{8,9},{9,8},{10,11... | collective-permute-start | bytes 589832 | tf_op jit(solution)/shard_map/ppermute | solution.py:314
  27.6 19.7 %all-to-all-start = ((f32[16,12,128]{2,1,0:T(8,128)}), f32[16,12,128]{2,1,0:T(8,128)S(1)}, u32[]{:S(2)}, u32[]{:S(2)}) async-start(f32[16,12,128]{2,1,0:T(8,128)} %get-tuple-element.39), calls=%async_computation | async-start | bytes 262144 | tf_op jit(solution)/shard_map/all_to_all | solution.py:321
  38.2 16.4 %collective-permute-start.4 = (bf16[128,768]{1,0:T(8,128)(2,1)S(1)}, bf16[128,768]{1,0:T(8,128)(2,1)S(1)}, u32[]{:S(2)}, u32[]{:S(2)}) collective-permute-start(bf16[128,768]{1,0:T(8,128)(2,1)S(1)} %get-tuple-element.31), channel_id=1, source_target_pairs={{0,16},{1,17},{2,18},{3,19},{4,20},{5,21},{6,22},{7,23},{8,24},{9,... | collective-permute-start | bytes 589832 | tf_op jit(solution)/shard_map/ppermute | solution.py:302
  39.8 14.8 %collective-permute-start.5 = (bf16[128,768]{1,0:T(8,128)(2,1)S(1)}, bf16[128,768]{1,0:T(8,128)(2,1)S(1)}, u32[]{:S(2)}, u32[]{:S(2)}) collective-permute-start(bf16[128,768]{1,0:T(8,128)(2,1)S(1)} %get-tuple-element.32), channel_id=1, source_target_pairs={{0,1},{1,0},{2,3},{3,2},{4,5},{5,4},{6,7},{7,6},{8,9},{9,8},{10,11... | collective-permute-start | bytes 589832 | tf_op jit(solution)/shard_map/ppermute | solution.py:314
  48.0 14.0 %all-to-all-start.1 = ((f32[16,12,128]{2,1,0:T(8,128)}), f32[16,12,128]{2,1,0:T(8,128)S(1)}, u32[]{:S(2)}, u32[]{:S(2)}) async-start(f32[16,12,128]{2,1,0:T(8,128)} %collect.1), calls=%async_computation.1 | async-start | bytes 262144 | tf_op jit(solution)/shard_map/all_to_all | solution.py:321
